TPU v7x, 256 devices: a whole 4x4x8 slice. The times are simulated.
256 devices in a mesh: segment: 4 (over y_hi, core), face: 64 (over x, z, y_lo).
Axes of the slice: x: 4, y: 4 (y_hi: 2, y_lo: 2; y = y_hi * 2 + y_lo), z: 8, core: 2. Of those that a mesh axis runs over, the one named last changes fastest.
Arguments:
- states: float32 [4, 9, 32768], P('segment', None, 'face'), may hold values from -6 to 6
- gru_state: float32 [4, 180, 8192], P('segment', None, 'face'), may hold values from -1 to 1
- neighbours: int32 [128, 4], P('face'), may hold values from 0 to 127, as said below
- orient: int32 [128, 4], P('face'), may hold values from 0 to 7
- embed_weight: bfloat16 [90, 9], replicated, may hold values from -2 to 2
- enc_fine_depth: bfloat16 [90, 49], replicated, may hold values from -0.875 to 0.875
- enc_fine_expand: bfloat16 [360, 90], replicated, may hold values from -0.625 to 0.625
- enc_fine_shrink: bfloat16 [90, 360], replicated, may hold values from -0.3125 to 0.3125
- down_weight: bfloat16 [180, 90], replicated, may hold values from -0.625 to 0.625
- encoder_rough_spatial_kernel: bfloat16 [180, 49], replicated, may hold values from -0.875 to 0.875
- enc_coarse_expand: bfloat16 [720, 180], replicated, may hold values from -0.4375 to 0.4375
- enc_coarse_shrink: bfloat16 [180, 720], replicated, may hold values from -0.21875 to 0.21875
- gru_weight: bfloat16 [3, 180, 360], replicated, may hold values from -0.3125 to 0.3125
- dec_coarse_depth: bfloat16 [180, 49], replicated, may hold values from -0.875 to 0.875
- dec_coarse_expand: bfloat16 [720, 180], replicated, may hold values from -0.4375 to 0.4375
- dec_coarse_shrink: bfloat16 [180, 720], replicated, may hold values from -0.21875 to 0.21875
- up_weight: bfloat16 [90, 180], replicated, may hold values from -0.4375 to 0.4375
- combine_weight: bfloat16 [90, 180], replicated, may hold values from -0.4375 to 0.4375
- dec_fine_depth: bfloat16 [90, 49], replicated, may hold values from -0.875 to 0.875
- dec_fine_expand: bfloat16 [360, 90], replicated, may hold values from -0.625 to 0.625
- dec_fine_shrink: bfloat16 [90, 360], replicated, may hold values from -0.3125 to 0.3125
- head_weight: bfloat16 [9, 90], replicated, may hold values from -0.625 to 0.625
Outputs:
- forecast: float32 [2, 4, 9, 32768], P(None, 'segment', None, 'face')
- gru_final: float32 [4, 180, 8192], P('segment', None, 'face')
Inputs may be any that keep to these rules, and one draw needn't show every extreme that they name: Tiles come in blocks of 2 consecutive ids, the blocks forming a closed loop; for a tile of block b, neighbours[t, 0] lies in block b - 1 and neighbours[t, 2] in block b + 1 (cyclically), neighbours[t, 1] and neighbours[t, 3] in block b.
All inputs are finite; a program needn't handle non-finite values.
Results may differ from a plain program's by a relative error of at most 0.025.
Values may be sent and summed in bfloat16 or wider, within the bound.
A program may use at most 64 MiB of HBM per device.

v0:
```python
import jax
import jax.numpy as jnp
from jax import lax
from jax.experimental import pallas as pl
from jax.experimental.pallas import tpu as pltpu
from jax.sharding import PartitionSpec as P

FIELDS = 9
C0 = 90
C1 = 180
SIDE0 = 16
SIDE1 = 8
TILES = 2
STEPS = 2
CELLS0 = TILES * SIDE0 * SIDE0
CELLS1 = TILES * SIDE1 * SIDE1
RIM0 = TILES * 3 * SIDE0
RIM1 = TILES * 3 * SIDE1
ROWS = 16
F32, BF16 = jnp.float32, jnp.bfloat16
NORTH, EAST, SOUTH, WEST = range(4)


def dot_nt(a, b):
    return lax.dot_general(a, b, (((1,), (1,)), ((), ())), preferred_element_type=F32)


def dot_nn(a, b):
    return jnp.dot(a, b, preferred_element_type=F32)


def one_hot(index, cells, axis):
    shape = (index.shape[0], cells) if axis == 1 else (cells, index.shape[1])
    hit = lax.broadcasted_iota(jnp.int32, shape, axis) == index
    return jnp.where(hit, 1.0, 0.0)


def rim_line(nbr, orient, tile, side, p):
    o = orient[tile, p]
    from_side = lax.shift_right_logical(o, 1)
    per_depth = jnp.where(
        from_side == 0, side, jnp.where(from_side == 1, -1, jnp.where(from_side == 2, -side, 1))
    )
    base = jnp.where(from_side == 1, side - 1, jnp.where(from_side == 2, side * (side - 1), 0))
    per_step = jnp.where((from_side & 1) == 0, 1, side)
    turned = (o & 1) == 1
    base = base + jnp.where(turned, per_step * (side - 1), 0)
    per_step = jnp.where(turned, -per_step, per_step)
    return base + (nbr[tile, p] & 1) * side * side, per_depth, per_step


def far_index(m, nbr, orient, side, p):
    index = jnp.full(m.shape, -1, jnp.int32)
    for tile in range(TILES):
        base, per_depth, per_step = rim_line(nbr, orient, tile, side, p)
        local = m - tile * 3 * side
        row = jnp.where(local >= 2 * side, 2, jnp.where(local >= side, 1, 0))
        depth = 2 - row if p == NORTH else row
        value = base + per_depth * depth + per_step * (local - row * side)
        index = jnp.where((local >= 0) & (local < 3 * side), value, index)
    return index


def near_index(nbr, orient, side):
    parts = []
    for tile in range(TILES):
        m = lax.broadcasted_iota(jnp.int32, (side * 8, 1), 0)
        row, place = lax.shift_right_logical(m, 3), m & 7
        base_e, depth_e, step_e = rim_line(nbr, orient, tile, side, EAST)
        base_w, depth_w, step_w = rim_line(nbr, orient, tile, side, WEST)
        east = base_e + depth_e * place + step_e * row
        west = base_w + depth_w * (7 - place) + step_w * row
        parts.append(jnp.where(place < 3, east, jnp.where(place >= 5, west, -1)))
    return jnp.concatenate(parts, 0)


def taps_first(weight, channels, lanes):
    wide = jnp.concatenate(
        [weight.astype(F32), jnp.zeros((channels, 128 - 49), F32)], 1
    )
    wide = jnp.concatenate([wide, jnp.zeros((lanes - channels, 128), F32)], 0)
    turned = wide.T[:49, :channels]
    return jnp.broadcast_to(turned[:, None, :], (49, 8, channels))


def normalise(y, channels):
    centred = y - jnp.sum(y, 1, keepdims=True) * (1.0 / channels)
    var = jnp.sum(centred * centred, 1, keepdims=True) * (1.0 / channels)
    return (centred * lax.rsqrt(var + 1e-6)).astype(BF16)


def gelu(x):
    return (0.5 * x) * (1.0 + lax.erf(x * 0.7071067811865476))


def finish(y, r, expand, shrink):
    normed = normalise(y, y.shape[1])
    expanded = gelu(dot_nt(normed, expand)).astype(BF16)
    return (r + dot_nt(expanded, shrink)).astype(BF16)


def conv_tile(pad, tile, rows, first, taps):
    total = None
    for q in range(7):
        x = pad[tile, :, first + q - 3 : first + q + 5, :]
        for u in range(7):
            term = taps[7 * u + q][None] * x[u : u + rows]
            total = term if total is None else total + term
    return total


def conv_halo(halo, side, tile, first, taps, rows):
    rows = list(rows)
    for q in range(7):
        for h in range(3):
            x = halo[side, tile, h, first + q - 3 : first + q + 5, :]
            for o in range(3):
                u = h - o if side == 0 else 6 + h - o
                if 0 <= u <= 6:
                    rows[o] = rows[o] + taps[7 * u + q] * x
    return rows


def kernel(
    states, gru_state, nbr, orient, embed_w, ef_depth, ef_expand, ef_shrink, down_w,
    ec_depth, ec_expand, ec_shrink, gru_w, dc_depth, dc_expand, dc_shrink,
    up_w, combine_w, df_depth, df_expand, df_shrink, head_w,
    forecast, gru_final,
    weather, carried, embed, gru_a, gru_b, comb_a, comb_b,
    taps_ef, taps_df, taps_ec, taps_dc,
    near0, near1, own_far, send0, send1, grow, pool,
    pad0, pad1, halo0, halo1, y0, y1, skip, merged,
    info_out, info_in, w_out, w_in, f_out, f_in, c_out, c_in,
    info_send, info_recv, w_send, w_recv, f_send, f_recv, c_send, c_recv,
):
    size = lax.axis_size("face")
    me = lax.axis_index("face")
    after, before = lax.rem(me + 1, size), lax.rem(me + size - 1, size)

    def pair(out, into, send, recv, slot=None):
        copies = []
        for way, target in enumerate((after, before)):
            src = out.at[way] if slot is None else out.at[slot, way]
            dst = into.at[way] if slot is None else into.at[slot, way]
            one = (way,) if slot is None else (slot, way)
            copies.append(
                pltpu.make_async_remote_copy(
                    src_ref=src, dst_ref=dst, send_sem=send.at[one], recv_sem=recv.at[one],
                    device_id={"face": target}, device_id_type=pl.DeviceIdType.MESH,
                )
            )
        return copies

    def start(copies):
        for copy in copies:
            copy.start()

    def wait(copies):
        for copy in copies:
            copy.wait()

    def weather_copies(step):
        copies = []
        for way, target in enumerate((after, before)):
            copies.append(
                pltpu.make_async_remote_copy(
                    src_ref=w_out.at[step], dst_ref=w_in.at[step, way],
                    send_sem=w_send.at[step, way], recv_sem=w_recv.at[step, way],
                    device_id={"face": target}, device_id_type=pl.DeviceIdType.MESH,
                )
            )
        return copies

    barrier = pltpu.get_barrier_semaphore()
    for target in (after, before):
        pl.semaphore_signal(
            barrier, inc=1, device_id={"face": target}, device_id_type=pl.DeviceIdType.MESH
        )

    weather[...] = jnp.zeros_like(weather)
    weather[:FIELDS] = states[0]
    w_out[0] = weather[...].astype(BF16)
    lane = lax.broadcasted_iota(jnp.int32, (1, 128), 1)
    for way, p in ((0, SOUTH), (1, NORTH)):
        info_out[way, 0:1] = far_index(lane, nbr, orient, SIDE0, p)
        info_out[way, 1:2] = far_index(lane, nbr, orient, SIDE1, p)
        info_out[way, 2:8] = jnp.zeros((6, 128), jnp.int32)
    pl.semaphore_wait(barrier, 2)
    info_copies = pair(info_out, info_in, info_send, info_recv)
    start(weather_copies(0))
    start(info_copies)

    embed[...] = jnp.zeros_like(embed)
    embed[:, :FIELDS] = embed_w[...].astype(F32)
    near0[...] = one_hot(near_index(nbr, orient, SIDE0), CELLS0, 1).astype(BF16)
    for way, p in ((0, NORTH), (1, SOUTH)):
        m = lax.broadcasted_iota(jnp.int32, (RIM0, 1), 0)
        own_far[way] = one_hot(far_index(m, nbr, orient, SIDE0, p), CELLS0, 1).astype(BF16)
    pad0[...] = jnp.zeros_like(pad0)
    halo0[...] = jnp.zeros_like(halo0)
    taps_ef[...] = taps_first(ef_depth[...], C0, 128)

    def prepare_rest():
        pad1[...] = jnp.zeros_like(pad1)
        halo1[...] = jnp.zeros_like(halo1)
        near1[...] = one_hot(near_index(nbr, orient, SIDE1), CELLS1, 1).astype(BF16)
        taps_df[...] = taps_first(df_depth[...], C0, 128)
        taps_ec[...] = taps_first(ec_depth[...], C1, 256)
        taps_dc[...] = taps_first(dc_depth[...], C1, 256)
        for g in range(3):
            wide = gru_w[g].astype(F32)
            gru_a[g] = wide[:, :C1].astype(BF16)
            gru_b[g] = wide[:, C1:].astype(BF16)
        wide = combine_w[...].astype(F32)
        comb_a[...] = wide[:, :C0].astype(BF16)
        comb_b[...] = wide[:, C0:].astype(BF16)

        def coarse_of(cell):
            tile = lax.shift_right_logical(cell, 8)
            row = lax.shift_right_logical(cell, 5) & 7
            return tile * 64 + row * 8 + (lax.shift_right_logical(cell, 1) & 7)

        cell = lax.broadcasted_iota(jnp.int32, (CELLS0, 1), 0)
        grow[...] = one_hot(coarse_of(cell), CELLS1, 1).astype(BF16)
        cell = lax.broadcasted_iota(jnp.int32, (1, CELLS0), 1)
        pool[...] = (0.25 * one_hot(coarse_of(cell), CELLS1, 0)).astype(BF16)
        state = jnp.concatenate([gru_state[0], jnp.zeros((256 - C1, CELLS1), F32)], 0)
        carried[...] = state.T[:, :C1]

    def prepare_sends():
        for way in range(2):
            wanted = info_in[1 - way]
            send0[way] = one_hot(wanted[0:1], CELLS0, 0).T[:RIM0].astype(BF16)
            send1[way] = one_hot(wanted[1:2], CELLS1, 0).T[:RIM1].astype(BF16)

    def fill0(r):
        pad0[:, 3 : 3 + SIDE0, 8:24, :] = r.astype(F32).reshape(TILES, SIDE0, SIDE0, C0)
        sides = dot_nn(near0[...], r).reshape(TILES, SIDE0, 8, C0)
        pad0[:, 3 : 3 + SIDE0, 0:8, :] = sides
        pad0[:, 3 : 3 + SIDE0, 24:32, :] = sides

    def fill1(r):
        pad1[:, 3 : 3 + SIDE1, 8:16, :] = r.astype(F32).reshape(TILES, SIDE1, SIDE1, C1)
        sides = dot_nn(near1[...], r).reshape(TILES, SIDE1, 8, C1)
        pad1[:, 3 : 3 + SIDE1, 0:8, :] = sides
        pad1[:, 3 : 3 + SIDE1, 16:24, :] = sides

    def fine_block_inner(taps, expand, shrink, out):
        def body(tile, _):
            for half in range(2):
                part = conv_tile(pad0, tile, SIDE0, 8 + 8 * half, taps)
                y0[tile, :, 8 * half : 8 * half + 8, :] = part
            y = y0[tile, 3:13].reshape(10 * SIDE0, C0)
            r = pad0[tile, 6:16, 8:24, :].reshape(10 * SIDE0, C0)
            out[tile, 3:13] = finish(y, r, expand[...], shrink[...]).reshape(10, SIDE0, C0)
            return 0

        lax.fori_loop(0, TILES, body, 0)

    def fine_block_outer(taps, expand, shrink, out):
        def body(tile, _):
            ys, rs = [], []
            for side, top in ((0, 0), (1, 13)):
                halves = []
                for half in range(2):
                    rows = [y0[tile, top + o, 8 * half : 8 * half + 8, :] for o in range(3)]
                    halves.append(conv_halo(halo0, side, tile, 8 + 8 * half, taps, rows))
                for o in range(3):
                    ys += [halves[0][o], halves[1][o]]
                rs.append(pad0[tile, top + 3 : top + 6, 8:24, :].reshape(3 * SIDE0, C0))
            y, r = jnp.concatenate(ys, 0), jnp.concatenate(rs, 0)
            done = finish(y, r, expand[...], shrink[...]).reshape(6, SIDE0, C0)
            out[tile, 0:3] = done[:3]
            out[tile, 13:16] = done[3:]
            return 0

        lax.fori_loop(0, TILES, body, 0)

    def coarse_block(r, slot, taps, expand, shrink):
        for way in range(2):
            c_out[slot, way] = dot_nn(send1[way], r).astype(BF16)
        copies = pair(c_out, c_in, c_send, c_recv, slot)
        start(copies)
        fill1(r)

        def body(tile, _):
            y1[tile] = conv_tile(pad1, tile, SIDE1, 8, taps)
            return 0

        lax.fori_loop(0, TILES, body, 0)
        wait(copies)
        for way in range(2):
            arrived = c_in[slot, way].astype(F32).reshape(TILES, 3, SIDE1, C1)
            halo1[way, :, :, 8:16, :] = arrived

        def edge(tile, _):
            for side, top in ((0, 0), (1, 5)):
                rows = [y1[tile, top + o] for o in range(3)]
                rows = conv_halo(halo1, side, tile, 8, taps, rows)
                for o in range(3):
                    y1[tile, top + o] = rows[o]
            return 0

        lax.fori_loop(0, TILES, edge, 0)
        y = y1[...].reshape(CELLS1, C1)
        return finish(y, r.astype(F32), expand[...], shrink[...])

    def step_body(step, _):
        fields = weather[...].astype(BF16).astype(F32).T.astype(BF16)
        lift = embed[...].astype(BF16)
        fill0(dot_nt(fields, lift).astype(BF16))
        fine_block_inner(taps_ef, ef_expand, ef_shrink, skip)

        @pl.when(step == 0)
        def _():
            prepare_rest()
            wait(info_copies)
            prepare_sends()

        wait(weather_copies(step))
        for way in range(2):
            rim = dot_nt(own_far[way], w_in[step, way]).astype(BF16)
            rim = dot_nt(rim, lift).astype(BF16).astype(F32)
            halo0[way, :, :, 8:24, :] = rim.reshape(TILES, 3, SIDE0, C0)
        fine_block_outer(taps_ef, ef_expand, ef_shrink, skip)

        kept = skip[...].reshape(CELLS0, C0)
        coarse = dot_nn(pool[...], kept).astype(BF16)
        coarse = dot_nt(coarse, down_w[...]).astype(BF16)
        coarse = coarse_block(coarse, 2 * step, taps_ec, ec_expand, ec_shrink)

        old = carried[...]
        held = old.astype(BF16)
        update = jax.nn.sigmoid(dot_nt(coarse, gru_a[0]) + dot_nt(held, gru_b[0]))
        reset = jax.nn.sigmoid(dot_nt(coarse, gru_a[1]) + dot_nt(held, gru_b[1]))
        gated = (reset * old).astype(BF16)
        candidate = jnp.tanh(dot_nt(coarse, gru_a[2]) + dot_nt(gated, gru_b[2]))
        new = (1.0 - update) * old + update * candidate
        carried[...] = new

        decoded = coarse_block(new.astype(BF16), 2 * step + 1, taps_dc, dc_expand, dc_shrink)

        lifted = dot_nt(decoded, up_w[...]).astype(BF16)
        lifted = dot_nn(grow[...], lifted).astype(BF16)
        joined = dot_nt(lifted, comb_a[...]) + dot_nt(kept, comb_b[...])
        joined = joined.astype(BF16)
        for way in range(2):
            f_out[step, way] = dot_nn(send0[way], joined).astype(BF16)
        copies = pair(f_out, f_in, f_send, f_recv, step)
        start(copies)
        fill0(joined)
        fine_block_inner(taps_df, df_expand, df_shrink, merged)
        wait(copies)
        for way in range(2):
            arrived = f_in[step, way].astype(F32).reshape(TILES, 3, SIDE0, C0)
            halo0[way, :, :, 8:24, :] = arrived
        fine_block_outer(taps_df, df_expand, df_shrink, merged)

        change = dot_nt(head_w[...], merged[...].reshape(CELLS0, C0))
        now = weather[:FIELDS] + change
        weather[:FIELDS] = now
        forecast[step, 0] = now

        @pl.when(step < STEPS - 1)
        def _():
            w_out[step + 1] = weather[...].astype(BF16)
            start(weather_copies(step + 1))

        return 0

    lax.fori_loop(0, STEPS, step_body, 0)
    last = jnp.concatenate([carried[...], jnp.zeros((CELLS1, 256 - C1), F32)], 1)
    gru_final[0] = last.T[:C1]


def local(states, gru_state, neighbours, orient, *weights):
    vmem = pl.BlockSpec(memory_space=pltpu.VMEM)
    smem = pl.BlockSpec(memory_space=pltpu.SMEM)
    scratch = [
        pltpu.VMEM((ROWS, CELLS0), F32),
        pltpu.VMEM((CELLS1, C1), F32),
        pltpu.VMEM((C0, ROWS), F32),
        pltpu.VMEM((3, C1, C1), BF16),
        pltpu.VMEM((3, C1, C1), BF16),
        pltpu.VMEM((C0, C0), BF16),
        pltpu.VMEM((C0, C0), BF16),
        pltpu.VMEM((49, 8, C0), F32),
        pltpu.VMEM((49, 8, C0), F32),
        pltpu.VMEM((49, 8, C1), F32),
        pltpu.VMEM((49, 8, C1), F32),
        pltpu.VMEM((TILES * SIDE0 * 8, CELLS0), BF16),
        pltpu.VMEM((TILES * SIDE1 * 8, CELLS1), BF16),
        pltpu.VMEM((2, RIM0, CELLS0), BF16),
        pltpu.VMEM((2, RIM0, CELLS0), BF16),
        pltpu.VMEM((2, RIM1, CELLS1), BF16),
        pltpu.VMEM((CELLS0, CELLS1), BF16),
        pltpu.VMEM((CELLS1, CELLS0), BF16),
        pltpu.VMEM((TILES, SIDE0 + 6, 32, C0), F32),
        pltpu.VMEM((TILES, SIDE1 + 6, 24, C1), F32),
        pltpu.VMEM((2, TILES, 3, 32, C0), F32),
        pltpu.VMEM((2, TILES, 3, 24, C1), F32),
        pltpu.VMEM((TILES, SIDE0, SIDE0, C0), F32),
        pltpu.VMEM((TILES, SIDE1, SIDE1, C1), F32),
        pltpu.VMEM((TILES, SIDE0, SIDE0, C0), BF16),
        pltpu.VMEM((TILES, SIDE0, SIDE0, C0), BF16),
        pltpu.VMEM((2, 8, 128), jnp.int32),
        pltpu.VMEM((2, 8, 128), jnp.int32),
        pltpu.VMEM((STEPS, ROWS, CELLS0), BF16),
        pltpu.VMEM((STEPS, 2, ROWS, CELLS0), BF16),
        pltpu.VMEM((STEPS, 2, RIM0, C0), BF16),
        pltpu.VMEM((STEPS, 2, RIM0, C0), BF16),
        pltpu.VMEM((2 * STEPS, 2, RIM1, C1), BF16),
        pltpu.VMEM((2 * STEPS, 2, RIM1, C1), BF16),
        pltpu.SemaphoreType.DMA((2,)),
        pltpu.SemaphoreType.DMA((2,)),
        pltpu.SemaphoreType.DMA((STEPS, 2)),
        pltpu.SemaphoreType.DMA((STEPS, 2)),
        pltpu.SemaphoreType.DMA((STEPS, 2)),
        pltpu.SemaphoreType.DMA((STEPS, 2)),
        pltpu.SemaphoreType.DMA((2 * STEPS, 2)),
        pltpu.SemaphoreType.DMA((2 * STEPS, 2)),
    ]
    return pl.pallas_call(
        kernel,
        out_shape=(
            jax.ShapeDtypeStruct((STEPS, 1, FIELDS, CELLS0), F32),
            jax.ShapeDtypeStruct((1, C1, CELLS1), F32),
        ),
        in_specs=[vmem, vmem, smem, smem] + [vmem] * len(weights),
        out_specs=(vmem, vmem),
        scratch_shapes=scratch,
        compiler_params=pltpu.CompilerParams(
            collective_id=0, has_side_effects=True, vmem_limit_bytes=48 * 1024 * 1024
        ),
    )(states, gru_state, neighbours, orient, *weights)


def solution(mesh):
    in_specs = (
        P("segment", None, "face"),
        P("segment", None, "face"),
        P("face", None),
        P("face", None),
    ) + (P(),) * 18
    out_specs = (P(None, "segment", None, "face"), P("segment", None, "face"))
    return jax.shard_map(local, mesh=mesh, in_specs=in_specs, out_specs=out_specs, check_vma=False)
```

profile of v0, /device:TPU:16, one launch (start us, length us, event | category | flops | bytes accessed | tf_op | source)
XLA Modules:
  0.0 70.8 jit_solution(16362379700395905096)
XLA Ops:
  0.6 0.8 %copy.26.embed_w = bf16[90,9]{1,0:T(8,128)(2,1)S(1)} copy(bf16[90,9]{0,1:T(8,128)(2,1)} %param.26) | data formatting | bytes 3240 | tf_op args[4]
  1.5 0.1 copy.27.ef_depth
  1.6 0.6 copy-done.20
  2.2 0.1 copy.35.df_depth
  2.3 0.6 copy-done.18
  2.9 0.7 %copy-done.16 = bf16[180,49]{0,1:T(8,128)(2,1)S(1)} copy-done((bf16[180,49]{0,1:T(8,128)(2,1)S(1)}, bf16[180,49]{0,1:T(8,128)(2,1)}, u32[]{:S(2)}) %copy-start.16) | copy-done | bytes 17664
  3.6 0.1 copy.29.ec_depth
  3.8 0.6 copy-done.17
  4.4 0.1 copy.31.dc_depth
  4.5 0.7 copy-done.14
  5.2 0.1 copy.33.up_w
  5.3 0.1 copy.34.combine_w
  5.4 0.6 copy-done.12
  6.1 0.1 copy.28.ef_expand
  6.2 0.1 copy.36.df_expand
  6.4 0.7 copy-done.9
  7.1 0.2 copy.30.ec_expand
  7.2 0.1 copy-done.10
  7.4 0.2 copy.32.dc_expand
  7.6 0.5 copy-done.1
  8.1 0.3 copy-done
  8.4 61.0 %shard_map.221 = (f32[2,1,9,512]{3,2,1,0:T(8,128)S(1)}, f32[1,180,128]{2,1,0:T(8,128)S(1)}) custom-call(f32[1,9,512]{2,1,0:T(8,128)S(1)} %copy.24.states, f32[1,180,128]{2,1,0:T(8,128)S(1)} %copy.25.gru_state, s32[2,4]{1,0:T(2,128)S(1)} %copy-done.7, s32[2,4]{1,0:T(2,128)S(1)} %copy-done.8, bf16[90,9]{1,0:T(8,128)(2,1)S(1)} %copy.26.embed_w, ...), custom_call_target="tpu_custom_call" | custom-call | tf_op jit(solution)/shard_map/pallas_call | solution.py:423
  69.5 0.7 copy.37
  70.1 0.7 %copy.38 = f32[1,180,128]{2,0,1:T(1,128)} copy(f32[1,180,128]{2,1,0:T(8,128)S(1)} %get-tuple-element.3) | data formatting | bytes 184320 | tf_op jit(solution)/shard_map/pallas_call | solution.py:423
  (34 shorter events, 0.2 us)
Async XLA Ops:
  0.6 0.8 %copy-start.19 = (bf16[90,49]{0,1:T(8,128)(2,1)S(1)}, bf16[90,49]{0,1:T(8,128)(2,1)}, u32[]{:S(2)}) copy-start(bf16[90,49]{0,1:T(8,128)(2,1)} %param.27) | copy-start | bytes 26464
  1.5 0.7 %copy-start.20 = (bf16[90,49]{0,1:T(8,128)(2,1)S(1)}, bf16[90,49]{0,1:T(8,128)(2,1)}, u32[]{:S(2)}) copy-start(bf16[90,49]{0,1:T(8,128)(2,1)} %param.40) | copy-start | bytes 26464
  2.2 0.7 %copy-start.18 = (f32[1,9,512]{2,0,1:T(1,128)S(1)}, f32[1,9,512]{2,0,1:T(1,128)}, u32[]{:S(2)}) copy-start(f32[1,9,512]{2,0,1:T(1,128)} %param.22) | copy-start | bytes 55300
  2.9 0.7 %copy-start.16 = (bf16[180,49]{0,1:T(8,128)(2,1)S(1)}, bf16[180,49]{0,1:T(8,128)(2,1)}, u32[]{:S(2)}) copy-start(bf16[180,49]{0,1:T(8,128)(2,1)} %param.31) | copy-start | bytes 52924
  3.6 0.7 %copy-start.17 = (bf16[180,49]{0,1:T(8,128)(2,1)S(1)}, bf16[180,49]{0,1:T(8,128)(2,1)}, u32[]{:S(2)}) copy-start(bf16[180,49]{0,1:T(8,128)(2,1)} %param.35) | copy-start | bytes 52924
  4.4 0.8 %copy-start.14 = (bf16[90,180]{0,1:T(8,128)(2,1)S(1)}, bf16[90,180]{0,1:T(8,128)(2,1)}, u32[]{:S(2)}) copy-start(bf16[90,180]{0,1:T(8,128)(2,1)} %param.38) | copy-start | bytes 97204
  4.4 0.9 %copy-start.15 = (bf16[90,180]{0,1:T(8,128)(2,1)S(1)}, bf16[90,180]{0,1:T(8,128)(2,1)}, u32[]{:S(2)}) copy-start(bf16[90,180]{0,1:T(8,128)(2,1)} %param.39) | copy-start | bytes 97204
  5.2 0.9 %copy-start.12 = (bf16[360,90]{0,1:T(8,128)(2,1)S(1)}, bf16[360,90]{0,1:T(8,128)(2,1)}, u32[]{:S(2)}) copy-start(bf16[360,90]{0,1:T(8,128)(2,1)} %param.28) | copy-start | bytes 194404
  5.2 1.0 %copy-start.13 = (bf16[360,90]{0,1:T(8,128)(2,1)S(1)}, bf16[360,90]{0,1:T(8,128)(2,1)}, u32[]{:S(2)}) copy-start(bf16[360,90]{0,1:T(8,128)(2,1)} %param.41) | copy-start | bytes 194404
  5.3 1.1 %copy-start.11 = (f32[1,180,128]{2,0,1:T(1,128)S(1)}, f32[1,180,128]{2,0,1:T(1,128)}, u32[]{:S(2)}) copy-start(f32[1,180,128]{2,0,1:T(1,128)} %param.23) | copy-start | bytes 276484
  6.1 1.0 %copy-start.9 = (bf16[720,180]{0,1:T(8,128)(2,1)S(1)}, bf16[720,180]{0,1:T(8,128)(2,1)}, u32[]{:S(2)}) copy-start(bf16[720,180]{0,1:T(8,128)(2,1)} %param.32) | copy-start | bytes 777604
  6.4 1.0 %copy-start.10 = (bf16[720,180]{0,1:T(8,128)(2,1)S(1)}, bf16[720,180]{0,1:T(8,128)(2,1)}, u32[]{:S(2)}) copy-start(bf16[720,180]{0,1:T(8,128)(2,1)} %param.36) | copy-start | bytes 777604
  7.1 1.0 %copy-start.1 = (bf16[180,720]{1,0:T(8,128)(2,1)S(1)}, bf16[180,720]{1,0:T(8,128)(2,1)}, u32[]{:S(2)}) copy-start(bf16[180,720]{1,0:T(8,128)(2,1)} %ec_shrink.1) | copy-start | bytes 777604
  7.1 1.1 %copy-start.2 = (bf16[180,720]{1,0:T(8,128)(2,1)S(1)}, bf16[180,720]{1,0:T(8,128)(2,1)}, u32[]{:S(2)}) copy-start(bf16[180,720]{1,0:T(8,128)(2,1)} %dc_shrink.1) | copy-start | bytes 777604
  7.3 1.0 %copy-start = (bf16[3,180,360]{2,1,0:T(8,128)(2,1)S(1)}, bf16[3,180,360]{2,1,0:T(8,128)(2,1)}, u32[]{:S(2)}) copy-start(bf16[3,180,360]{2,1,0:T(8,128)(2,1)} %gru_w.1) | copy-start | bytes 1166404
  7.4 1.1 %copy-start.3 = (bf16[90,360]{1,0:T(8,128)(2,1)S(1)}, bf16[90,360]{1,0:T(8,128)(2,1)}, u32[]{:S(2)}) copy-start(bf16[90,360]{1,0:T(8,128)(2,1)} %ef_shrink.1) | copy-start | bytes 194404
  7.4 1.1 %copy-start.4 = (bf16[90,360]{1,0:T(8,128)(2,1)S(1)}, bf16[90,360]{1,0:T(8,128)(2,1)}, u32[]{:S(2)}) copy-start(bf16[90,360]{1,0:T(8,128)(2,1)} %df_shrink.1) | copy-start | bytes 194404
  7.4 1.1 %copy-start.5 = (bf16[180,90]{1,0:T(8,128)(2,1)S(1)}, bf16[180,90]{1,0:T(8,128)(2,1)}, u32[]{:S(2)}) copy-start(bf16[180,90]{1,0:T(8,128)(2,1)} %down_w.1) | copy-start | bytes 97204
  7.4 1.1 %copy-start.6 = (bf16[9,90]{1,0:T(8,128)(2,1)S(1)}, bf16[9,90]{1,0:T(8,128)(2,1)}, u32[]{:S(2)}) copy-start(bf16[9,90]{1,0:T(8,128)(2,1)} %head_w.1) | copy-start | bytes 4864
  7.4 1.1 %copy-start.7 = (s32[2,4]{1,0:T(2,128)S(1)}, s32[2,4]{1,0:T(2,128)}, u32[]{:S(2)}) copy-start(s32[2,4]{1,0:T(2,128)} %nbr.1) | copy-start | bytes 100
  7.4 1.1 %copy-start.8 = (s32[2,4]{1,0:T(2,128)S(1)}, s32[2,4]{1,0:T(2,128)}, u32[]{:S(2)}) copy-start(s32[2,4]{1,0:T(2,128)} %orient.1) | copy-start | bytes 100
where the time goes:
time: 71.3 us; the launch traced here: 70.8 us
  Pallas kernels  61 us (86%)
  local copies, waits for them, and re-layouts  9.09 us (13%)
  between operations  0.75 us (1%)
    pallas_call x1, Pallas kernels, local(): pl.pallas_call(kernel, out_shape=(jax.ShapeDtypeStruct((STEPS, 1, FIELDS,...  61 us
    unnamed x55, local copies, waits for them, and re-layouts  7.7 us

commit v1 on v0

v1 whole, which is shorter than its diff:
```python
import jax
import jax.numpy as jnp
from jax import lax
from jax.experimental import pallas as pl
from jax.experimental.pallas import tpu as pltpu
from jax.sharding import PartitionSpec as P

FIELDS = 9
C0 = 90
C1 = 180
SIDE0 = 16
SIDE1 = 8
TILES = 2
STEPS = 2
CELLS0 = TILES * SIDE0 * SIDE0
CELLS1 = TILES * SIDE1 * SIDE1
RIM0 = TILES * 3 * SIDE0
RIM1 = TILES * 3 * SIDE1
ROWS = 16
F32, BF16 = jnp.float32, jnp.bfloat16
NORTH, EAST, SOUTH, WEST = range(4)


def dot_nt(a, b):
    return lax.dot_general(a, b, (((1,), (1,)), ((), ())), preferred_element_type=F32)


def dot_nn(a, b):
    return jnp.dot(a, b, preferred_element_type=F32)


def one_hot(index, cells, axis):
    shape = (index.shape[0], cells) if axis == 1 else (cells, index.shape[1])
    hit = lax.broadcasted_iota(jnp.int32, shape, axis) == index
    return jnp.where(hit, 1.0, 0.0)


def rim_line(nbr, orient, tile, side, p):
    o = orient[tile, p]
    from_side = lax.shift_right_logical(o, 1)
    per_depth = jnp.where(
        from_side == 0, side, jnp.where(from_side == 1, -1, jnp.where(from_side == 2, -side, 1))
    )
    base = jnp.where(from_side == 1, side - 1, jnp.where(from_side == 2, side * (side - 1), 0))
    per_step = jnp.where((from_side & 1) == 0, 1, side)
    turned = (o & 1) == 1
    base = base + jnp.where(turned, per_step * (side - 1), 0)
    per_step = jnp.where(turned, -per_step, per_step)
    return base + (nbr[tile, p] & 1) * side * side, per_depth, per_step


def far_index(m, nbr, orient, side, p):
    index = jnp.full(m.shape, -1, jnp.int32)
    for tile in range(TILES):
        base, per_depth, per_step = rim_line(nbr, orient, tile, side, p)
        local = m - tile * 3 * side
        row = jnp.where(local >= 2 * side, 2, jnp.where(local >= side, 1, 0))
        depth = 2 - row if p == NORTH else row
        value = base + per_depth * depth + per_step * (local - row * side)
        index = jnp.where((local >= 0) & (local < 3 * side), value, index)
    return index


def near_index(nbr, orient, side):
    parts = []
    for tile in range(TILES):
        m = lax.broadcasted_iota(jnp.int32, (side * 8, 1), 0)
        row, place = lax.shift_right_logical(m, 3), m & 7
        base_e, depth_e, step_e = rim_line(nbr, orient, tile, side, EAST)
        base_w, depth_w, step_w = rim_line(nbr, orient, tile, side, WEST)
        east = base_e + depth_e * place + step_e * row
        west = base_w + depth_w * (7 - place) + step_w * row
        parts.append(jnp.where(place < 3, east, jnp.where(place >= 5, west, -1)))
    return jnp.concatenate(parts, 0)


def spread_taps(weight):
    return jnp.broadcast_to(weight.astype(F32)[:, None, :], (49, 8, weight.shape[1]))


def halves(x):
    high = x.astype(BF16)
    return jnp.concatenate([high, (x - high.astype(F32)).astype(BF16)], 0)


def normalise(y, channels):
    centred = y - jnp.sum(y, 1, keepdims=True) * (1.0 / channels)
    var = jnp.sum(centred * centred, 1, keepdims=True) * (1.0 / channels)
    return (centred * lax.rsqrt(var + 1e-6)).astype(BF16)


def gelu(x):
    return (0.5 * x) * (1.0 + lax.erf(x * 0.7071067811865476))


def finish(y, r, expand, shrink):
    normed = normalise(y, y.shape[1])
    expanded = gelu(dot_nn(normed, expand)).astype(BF16)
    return (r + dot_nt(expanded, shrink)).astype(BF16)


def conv_tile(pad, tile, rows, first, taps):
    total = None
    for q in range(7):
        x = pad[tile, :, first + q - 3 : first + q + 5, :]
        for u in range(7):
            term = taps[7 * u + q][None] * x[u : u + rows]
            total = term if total is None else total + term
    return total


def conv_halo(halo, side, tile, first, taps, rows):
    rows = list(rows)
    for q in range(7):
        for h in range(3):
            x = halo[side, tile, h, first + q - 3 : first + q + 5, :]
            for o in range(3):
                u = h - o if side == 0 else 6 + h - o
                if 0 <= u <= 6:
                    rows[o] = rows[o] + taps[7 * u + q] * x
    return rows


WEIGHTS = 18


def kernel(
    states, gru_state, nbr, orient, *refs,
):
    hbm_weights, refs = refs[:WEIGHTS], refs[WEIGHTS:]
    forecast, gru_final = refs[:2]
    (
        embed_w, ef_depth, ef_expand, ef_shrink, down_w, ec_depth, ec_expand, ec_shrink,
        gru_w, dc_depth, dc_expand, dc_shrink, up_w, combine_w, df_depth, df_expand,
        df_shrink, head_w,
    ) = vmem_weights = refs[2 : 2 + WEIGHTS]
    (
        states_in, gru_in,
        weather, carried, embed, gru_a, gru_b, lift_w, comb_b,
        taps_ef, taps_df, taps_ec, taps_dc,
        near0, near1, own_far, far1, far0, grow, gather, far_grow,
        pad0, pad1, halo0, halo1, y0, y1, edge_y, edge_r, skip, merged,
        part, far_part, held_gates,
        info_out, info_in, w_out, w_in, f_out, f_in, c_out, c_in,
        load,
        info_send, info_recv, w_send, w_recv, f_send, f_recv, c_send, c_recv,
    ) = refs[2 + WEIGHTS :]
    size = lax.axis_size("face")
    me = lax.axis_index("face")
    after, before = lax.rem(me + 1, size), lax.rem(me + size - 1, size)

    def remote(src, dst, send, recv, target):
        return pltpu.make_async_remote_copy(
            src_ref=src, dst_ref=dst, send_sem=send, recv_sem=recv,
            device_id={"face": target}, device_id_type=pl.DeviceIdType.MESH,
        )

    def pair(out, into, send, recv, slot):
        return [
            remote(out.at[slot, w], into.at[slot, w], send.at[slot, w], recv.at[slot, w], target)
            for w, target in enumerate((after, before))
        ]

    def info_copies():
        return [
            remote(info_out.at[w], info_in.at[w], info_send.at[w], info_recv.at[w], target)
            for w, target in enumerate((after, before))
        ]

    def weather_copies(step):
        return [
            remote(w_out.at[step], w_in.at[step, w], w_send.at[step, w], w_recv.at[step, w], target)
            for w, target in enumerate((after, before))
        ]

    def start(copies):
        for copy in copies:
            copy.start()

    def wait(copies):
        for copy in copies:
            copy.wait()

    barrier = pltpu.get_barrier_semaphore()
    for target in (after, before):
        pl.semaphore_signal(
            barrier, inc=1, device_id={"face": target}, device_id_type=pl.DeviceIdType.MESH
        )
    loads = [pltpu.make_async_copy(states, states_in, load.at[0])]
    loads += [
        pltpu.make_async_copy(src, dst, load.at[2 + n])
        for n, (src, dst) in enumerate(zip(hbm_weights, vmem_weights))
    ]
    loads.append(pltpu.make_async_copy(gru_state, gru_in, load.at[1]))
    start(loads)

    lane = lax.broadcasted_iota(jnp.int32, (1, 128), 1)
    for way, p in ((0, SOUTH), (1, NORTH)):
        info_out[way, 0:1] = far_index(lane, nbr, orient, SIDE0, p)
        info_out[way, 1:2] = far_index(lane, nbr, orient, SIDE1, p)
        info_out[way, 2:8] = jnp.zeros((6, 128), jnp.int32)
    weather[...] = jnp.zeros_like(weather)
    loads[0].wait()
    weather[:FIELDS] = states_in[:, 0, :]
    w_out[0] = weather[...].astype(BF16)
    pl.semaphore_wait(barrier, 2)
    start(weather_copies(0))
    start(info_copies())

    near0[...] = one_hot(near_index(nbr, orient, SIDE0), CELLS0, 1).astype(BF16)
    for way, p in ((0, NORTH), (1, SOUTH)):
        m = lax.broadcasted_iota(jnp.int32, (RIM0, 1), 0)
        own_far[way] = one_hot(far_index(m, nbr, orient, SIDE0, p), CELLS0, 1).astype(BF16)
    pad0[...] = jnp.zeros_like(pad0)
    halo0[...] = jnp.zeros_like(halo0)
    for copy in loads[1:]:
        copy.wait()
    embed[...] = jnp.zeros_like(embed)
    embed[:FIELDS] = embed_w[...].astype(F32)
    taps_ef[...] = spread_taps(ef_depth[...])

    def prepare_rest():
        pad1[...] = jnp.zeros_like(pad1)
        halo1[...] = jnp.zeros_like(halo1)
        near1[...] = one_hot(near_index(nbr, orient, SIDE1), CELLS1, 1).astype(BF16)
        taps_df[...] = spread_taps(df_depth[...])
        taps_ec[...] = spread_taps(ec_depth[...])
        taps_dc[...] = spread_taps(dc_depth[...])
        for g in range(3):
            wide = gru_w[g].astype(F32)
            gru_a[g] = wide[:, :C1].astype(BF16)
            gru_b[g] = wide[:, C1:].astype(BF16)
        wide = combine_w[...].astype(F32)
        comb_b[...] = wide[C0:].astype(BF16)
        lift_w[...] = dot_nn(up_w[...], wide[:C0].astype(BF16)).astype(BF16)

        def coarse_of(cell):
            tile = lax.shift_right_logical(cell, 8)
            row = lax.shift_right_logical(cell, 5) & 7
            return tile * 64 + row * 8 + (lax.shift_right_logical(cell, 1) & 7)

        cell = lax.broadcasted_iota(jnp.int32, (CELLS0, 1), 0)
        one = one_hot(coarse_of(cell), CELLS1, 1).astype(BF16)
        grow[:, :CELLS1] = one
        grow[:, CELLS1:] = one
        cell = lax.broadcasted_iota(jnp.int32, (1, CELLS0), 1)
        gather[:CELLS1] = (0.25 * one_hot(coarse_of(cell), CELLS1, 0)).astype(BF16)
        state = jnp.concatenate(
            [gru_in[...].reshape(C1, CELLS1), jnp.zeros((256 - C1, CELLS1), F32)], 0
        )
        carried[...] = state.T[:, :C1]

    def prepare_sends():
        for way in range(2):
            wanted = info_in[1 - way]
            rows = slice(way * RIM0, (way + 1) * RIM0)
            far0[rows] = one_hot(wanted[0:1], CELLS0, 0).T[:RIM0].astype(BF16)
            rows = slice(way * RIM1, (way + 1) * RIM1)
            far1[rows] = one_hot(wanted[1:2], CELLS1, 0).T[:RIM1].astype(BF16)
        gather[CELLS1:] = dot_nn(far1[...], gather[:CELLS1]).astype(BF16)
        one = dot_nn(far0[...], grow[:, :CELLS1]).astype(BF16)
        far_grow[:, :CELLS1] = one
        far_grow[:, CELLS1:] = one

    def fill0(r):
        pad0[:, 3 : 3 + SIDE0, 8:24, :] = r.astype(F32).reshape(TILES, SIDE0, SIDE0, C0)
        sides = dot_nn(near0[...], r).reshape(TILES, SIDE0, 8, C0)
        pad0[:, 3 : 3 + SIDE0, 0:8, :] = sides
        pad0[:, 3 : 3 + SIDE0, 24:32, :] = sides

    def fill1(r):
        pad1[:, 3 : 3 + SIDE1, 8:16, :] = r.astype(F32).reshape(TILES, SIDE1, SIDE1, C1)
        sides = dot_nn(near1[...], r).reshape(TILES, SIDE1, 8, C1)
        pad1[:, 3 : 3 + SIDE1, 0:8, :] = sides
        pad1[:, 3 : 3 + SIDE1, 16:24, :] = sides

    def fine_block_inner(taps, expand, shrink, out):
        def body(tile, _):
            for half in range(2):
                total = conv_tile(pad0, tile, SIDE0, 8 + 8 * half, taps)
                y0[tile, :, 8 * half : 8 * half + 8, :] = total
            y = y0[tile, 3:13].reshape(10 * SIDE0, C0)
            r = pad0[tile, 6:16, 8:24, :].reshape(10 * SIDE0, C0)
            out[tile, 3:13] = finish(y, r, expand[...], shrink[...]).reshape(10, SIDE0, C0)
            return 0

        lax.fori_loop(0, TILES, body, 0)
        for tile in range(TILES):
            for side, top in ((0, 3), (1, 16)):
                edge_r[tile, side] = pad0[tile, top : top + 3, 8:24, :]

    def fine_block_outer(taps, expand, shrink, out):
        def body(tile, _):
            for side, top in ((0, 0), (1, 13)):
                for half in range(2):
                    columns = slice(8 * half, 8 * half + 8)
                    rows = [y0[tile, top + o, columns, :] for o in range(3)]
                    rows = conv_halo(halo0, side, tile, 8 + 8 * half, taps, rows)
                    for o in range(3):
                        edge_y[tile, side, o, columns, :] = rows[o]
            return 0

        lax.fori_loop(0, TILES, body, 0)
        y = edge_y[...].reshape(2 * RIM0, C0)
        r = edge_r[...].reshape(2 * RIM0, C0)
        done = finish(y, r, expand[...], shrink[...]).reshape(TILES, 2, 3, SIDE0, C0)
        for tile in range(TILES):
            out[tile, 0:3] = done[tile, 0]
            out[tile, 13:16] = done[tile, 1]

    def coarse_block(r, slot, taps, expand, shrink, meanwhile):
        copies = pair(c_out, c_in, c_send, c_recv, slot)
        start(copies)
        fill1(r)

        def body(tile, _):
            y1[tile] = conv_tile(pad1, tile, SIDE1, 8, taps)
            return 0

        lax.fori_loop(0, TILES, body, 0)
        meanwhile()
        wait(copies)
        for way in range(2):
            arrived = c_in[slot, way].astype(F32).reshape(TILES, 3, SIDE1, C1)
            halo1[way, :, :, 8:16, :] = arrived

        def edge(tile, _):
            for side, top in ((0, 0), (1, 5)):
                rows = [y1[tile, top + o] for o in range(3)]
                rows = conv_halo(halo1, side, tile, 8, taps, rows)
                for o in range(3):
                    y1[tile, top + o] = rows[o]
            return 0

        lax.fori_loop(0, TILES, edge, 0)
        y = y1[...].reshape(CELLS1, C1)
        return finish(y, r.astype(F32), expand[...], shrink[...])

    def step_body(step, _):
        fields = weather[...].astype(BF16).astype(F32).T.astype(BF16)
        lift = embed[...].astype(BF16)
        fill0(dot_nn(fields, lift).astype(BF16))
        fine_block_inner(taps_ef, ef_expand, ef_shrink, skip)

        @pl.when(step == 0)
        def _():
            prepare_rest()
            wait(info_copies())
            prepare_sends()

        wait(weather_copies(step))
        for way in range(2):
            rim = dot_nt(own_far[way], w_in[step, way]).astype(BF16)
            rim = dot_nn(rim, lift).astype(BF16).astype(F32)
            halo0[way, :, :, 8:24, :] = rim.reshape(TILES, 3, SIDE0, C0)
        fine_block_outer(taps_ef, ef_expand, ef_shrink, skip)

        coarse = dot_nn(gather[...], skip[...].reshape(CELLS0, C0)).astype(BF16)
        coarse = dot_nt(coarse, down_w[...]).astype(BF16)
        for way in range(2):
            top = CELLS1 + way * RIM1
            c_out[2 * step, way] = coarse[top : top + RIM1]

        def after_skip():
            kept = skip[...].reshape(CELLS0, C0)
            part[...] = dot_nn(kept, comb_b[...])
            far_part[...] = dot_nn(dot_nn(far0[...], kept).astype(BF16), comb_b[...])
            held = carried[...].astype(BF16)
            for g in range(2):
                held_gates[g] = dot_nt(held, gru_b[g])

        coarse = coarse_block(
            coarse[:CELLS1], 2 * step, taps_ec, ec_expand, ec_shrink, after_skip
        )

        old = carried[...]
        update = jax.nn.sigmoid(dot_nt(coarse, gru_a[0]) + held_gates[0])
        reset = jax.nn.sigmoid(dot_nt(coarse, gru_a[1]) + held_gates[1])
        gated = (reset * old).astype(BF16)
        candidate = jnp.tanh(dot_nt(coarse, gru_a[2]) + dot_nt(gated, gru_b[2]))
        new = (1.0 - update) * old + update * candidate
        carried[...] = new

        new = new.astype(BF16)
        wanted = dot_nn(far1[...], new).astype(BF16)
        for way in range(2):
            c_out[2 * step + 1, way] = wanted[way * RIM1 : (way + 1) * RIM1]

        def after_update():
            @pl.when(step == STEPS - 1)
            def _():
                last = jnp.concatenate([carried[...], jnp.zeros((CELLS1, 256 - C1), F32)], 1)
                gru_final[0] = last.T[:C1]

        decoded = coarse_block(
            new, 2 * step + 1, taps_dc, dc_expand, dc_shrink, after_update
        )

        lifted = halves(dot_nn(decoded, lift_w[...]))
        wanted = (dot_nn(far_grow[...], lifted) + far_part[...]).astype(BF16)
        for way in range(2):
            f_out[step, way] = wanted[way * RIM0 : (way + 1) * RIM0]
        copies = pair(f_out, f_in, f_send, f_recv, step)
        start(copies)
        fill0((dot_nn(grow[...], lifted) + part[...]).astype(BF16))
        fine_block_inner(taps_df, df_expand, df_shrink, merged)
        wait(copies)
        for way in range(2):
            arrived = f_in[step, way].astype(F32).reshape(TILES, 3, SIDE0, C0)
            halo0[way, :, :, 8:24, :] = arrived
        fine_block_outer(taps_df, df_expand, df_shrink, merged)

        change = dot_nt(head_w[...], merged[...].reshape(CELLS0, C0))
        now = weather[:FIELDS] + change
        weather[:FIELDS] = now

        @pl.when(step < STEPS - 1)
        def _():
            w_out[step + 1] = weather[...].astype(BF16)
            start(weather_copies(step + 1))

        forecast[step, 0] = now
        return 0

    lax.fori_loop(0, STEPS, step_body, 0)


def local(states, gru_state, neighbours, orient, *weights):
    (
        embed_w, ef_depth, ef_expand, ef_shrink, down_w, ec_depth, ec_expand, ec_shrink,
        gru_w, dc_depth, dc_expand, dc_shrink, up_w, combine_w, df_depth, df_expand,
        df_shrink, head_w,
    ) = weights
    weights = (
        embed_w.T, ef_depth.T, ef_expand.T, ef_shrink, down_w, ec_depth.T, ec_expand.T, ec_shrink,
        gru_w, dc_depth.T, dc_expand.T, dc_shrink, up_w.T, combine_w.T, df_depth.T, df_expand.T,
        df_shrink, head_w,
    )
    hbm = pl.BlockSpec(memory_space=pltpu.HBM)
    smem = pl.BlockSpec(memory_space=pltpu.SMEM)
    scratch = [pltpu.VMEM(w.shape, w.dtype) for w in weights]
    scratch += [
        pltpu.VMEM((FIELDS, 1, CELLS0), F32),
        pltpu.VMEM((C1, 1, CELLS1), F32),
        pltpu.VMEM((ROWS, CELLS0), F32),
        pltpu.VMEM((CELLS1, C1), F32),
        pltpu.VMEM((ROWS, C0), F32),
        pltpu.VMEM((3, C1, C1), BF16),
        pltpu.VMEM((3, C1, C1), BF16),
        pltpu.VMEM((C1, C0), BF16),
        pltpu.VMEM((C0, C0), BF16),
        pltpu.VMEM((49, 8, C0), F32),
        pltpu.VMEM((49, 8, C0), F32),
        pltpu.VMEM((49, 8, C1), F32),
        pltpu.VMEM((49, 8, C1), F32),
        pltpu.VMEM((TILES * SIDE0 * 8, CELLS0), BF16),
        pltpu.VMEM((TILES * SIDE1 * 8, CELLS1), BF16),
        pltpu.VMEM((2, RIM0, CELLS0), BF16),
        pltpu.VMEM((2 * RIM1, CELLS1), BF16),
        pltpu.VMEM((2 * RIM0, CELLS0), BF16),
        pltpu.VMEM((CELLS0, 2 * CELLS1), BF16),
        pltpu.VMEM((CELLS1 + 2 * RIM1, CELLS0), BF16),
        pltpu.VMEM((2 * RIM0, 2 * CELLS1), BF16),
        pltpu.VMEM((TILES, SIDE0 + 6, 32, C0), F32),
        pltpu.VMEM((TILES, SIDE1 + 6, 24, C1), F32),
        pltpu.VMEM((2, TILES, 3, 32, C0), F32),
        pltpu.VMEM((2, TILES, 3, 24, C1), F32),
        pltpu.VMEM((TILES, SIDE0, SIDE0, C0), F32),
        pltpu.VMEM((TILES, SIDE1, SIDE1, C1), F32),
        pltpu.VMEM((TILES, 2, 3, SIDE0, C0), F32),
        pltpu.VMEM((TILES, 2, 3, SIDE0, C0), F32),
        pltpu.VMEM((TILES, SIDE0, SIDE0, C0), BF16),
        pltpu.VMEM((TILES, SIDE0, SIDE0, C0), BF16),
        pltpu.VMEM((CELLS0, C0), F32),
        pltpu.VMEM((2 * RIM0, C0), F32),
        pltpu.VMEM((2, CELLS1, C1), F32),
        pltpu.VMEM((2, 8, 128), jnp.int32),
        pltpu.VMEM((2, 8, 128), jnp.int32),
        pltpu.VMEM((STEPS, ROWS, CELLS0), BF16),
        pltpu.VMEM((STEPS, 2, ROWS, CELLS0), BF16),
        pltpu.VMEM((STEPS, 2, RIM0, C0), BF16),
        pltpu.VMEM((STEPS, 2, RIM0, C0), BF16),
        pltpu.VMEM((2 * STEPS, 2, RIM1, C1), BF16),
        pltpu.VMEM((2 * STEPS, 2, RIM1, C1), BF16),
        pltpu.SemaphoreType.DMA((2 + WEIGHTS,)),
        pltpu.SemaphoreType.DMA((2,)),
        pltpu.SemaphoreType.DMA((2,)),
        pltpu.SemaphoreType.DMA((STEPS, 2)),
        pltpu.SemaphoreType.DMA((STEPS, 2)),
        pltpu.SemaphoreType.DMA((STEPS, 2)),
        pltpu.SemaphoreType.DMA((STEPS, 2)),
        pltpu.SemaphoreType.DMA((2 * STEPS, 2)),
        pltpu.SemaphoreType.DMA((2 * STEPS, 2)),
    ]
    return pl.pallas_call(
        kernel,
        out_shape=(
            jax.ShapeDtypeStruct((STEPS, 1, FIELDS, CELLS0), F32),
            jax.ShapeDtypeStruct((1, C1, CELLS1), F32),
        ),
        in_specs=[hbm, hbm, smem, smem] + [hbm] * len(weights),
        out_specs=(pl.BlockSpec(memory_space=pltpu.VMEM),) * 2,
        scratch_shapes=scratch,
        compiler_params=pltpu.CompilerParams(
            collective_id=0, has_side_effects=True, vmem_limit_bytes=56 * 1024 * 1024
        ),
    )(states.transpose(1, 0, 2), gru_state.transpose(1, 0, 2), neighbours, orient, *weights)


def solution(mesh):
    in_specs = (
        P("segment", None, "face"),
        P("segment", None, "face"),
        P("face", None),
        P("face", None),
    ) + (P(),) * 18
    out_specs = (P(None, "segment", None, "face"), P("segment", None, "face"))
    return jax.shard_map(local, mesh=mesh, in_specs=in_specs, out_specs=out_specs, check_vma=False)
```

time: 71.3 us -> 62.6 us (0.88)
  local copies, waits for them, and re-layouts: 9.09 us -> 2.26 us
  Pallas kernels: 61 us -> 59.6 us
    unnamed x55 -> x2, local copies, waits for them, and re-layouts: 7.7 us -> 0.01 us
    pallas_call x1, Pallas kernels: 61 us -> 59.6 us  [local(): pl.pallas_call(kernel, out_shape=(jax.ShapeDtypeStruct((STEPS, 1, FIELDS,...]
    pallas_call x2, local copies, waits for them, and re-layouts: 1.39 us -> 2.26 us  [local(): pl.pallas_call(kernel, out_shape=(jax.ShapeDtypeStruct((STEPS, 1, FIELDS,...]
where the time goes in v1:
time: 62.6 us; the launch traced here: 62.5 us
  Pallas kernels  59.6 us (95%)
  local copies, waits for them, and re-layouts  2.26 us (4%)
  between operations  0.66 us (1%)
    pallas_call x1, Pallas kernels, local(): pl.pallas_call(kernel, out_shape=(jax.ShapeDtypeStruct((STEPS, 1, FIELDS,...  59.6 us
    pallas_call x2, local copies, waits for them, and re-layouts, local(): pl.pallas_call(kernel, out_shape=(jax.ShapeDtypeStruct((STEPS, 1, FIELDS,...  2.26 us

profile of v1, /device:TPU:16, one launch (start us, length us, event | category | flops | bytes accessed | tf_op | source)
XLA Modules:
  0.0 62.5 jit_solution(17819076462042191205)
XLA Ops:
  0.6 59.6 %shard_map.221 = (f32[2,1,9,512]{3,2,1,0:T(8,128)}, f32[1,180,128]{2,1,0:T(8,128)}) custom-call(f32[9,1,512]{2,1,0:T(1,128)} %bitcast.22, f32[180,1,128]{2,1,0:T(1,128)} %bitcast.15, s32[2,4]{1,0:T(2,128)} %nbr.1, s32[2,4]{1,0:T(2,128)} %orient.1, bf16[9,90]{1,0:T(8,128)(2,1)} %bitcast.25, bf16[49,90]{1,0:T(8,128)(2,1)} %bitcast.23, ...), custom_call_target="tpu_custom_call" | custom-call | tf_op jit(solution)/shard_map/pallas_call | solution.py:495
  60.2 0.0 copy-start
  60.2 1.5 %copy.24 = f32[2,1,9,512]{3,1,2,0:T(1,128)} copy(f32[2,1,9,512]{3,2,1,0:T(8,128)} %get-tuple-element.2) | data formatting | bytes 73728 | tf_op jit(solution)/shard_map/pallas_call | solution.py:495
  61.8 0.0 copy-done
  61.8 0.7 %copy.25 = f32[1,180,128]{2,0,1:T(1,128)} copy(f32[1,180,128]{2,1,0:T(8,128)S(1)} %copy-done) | data formatting | bytes 184320 | tf_op jit(solution)/shard_map/pallas_call | solution.py:495
Async XLA Ops:
  60.2 1.5 %copy-start = (f32[1,180,128]{2,1,0:T(8,128)S(1)}, f32[1,180,128]{2,1,0:T(8,128)}, u32[]{:S(2)}) copy-start(f32[1,180,128]{2,1,0:T(8,128)} %get-tuple-element.3) | copy-start | bytes 276484

commit v2 on v1

--- a/solution.py
+++ b/solution.py
@@ -19,6 +19,7 @@
 ROWS = 16
 F32, BF16 = jnp.float32, jnp.bfloat16
 NORTH, EAST, SOUTH, WEST = range(4)
+ROW = 16
 
 
 def dot_nt(a, b):
@@ -61,17 +62,28 @@
     return index
 
 
-def near_index(nbr, orient, side):
-    parts = []
+def near_index(m, nbr, orient, side):
+    index = jnp.full(m.shape, -1, jnp.int32)
     for tile in range(TILES):
-        m = lax.broadcasted_iota(jnp.int32, (side * 8, 1), 0)
-        row, place = lax.shift_right_logical(m, 3), m & 7
         base_e, depth_e, step_e = rim_line(nbr, orient, tile, side, EAST)
         base_w, depth_w, step_w = rim_line(nbr, orient, tile, side, WEST)
+        local = m - tile * side * 8
+        row, place = lax.shift_right_arithmetic(local, 3), local & 7
         east = base_e + depth_e * place + step_e * row
         west = base_w + depth_w * (7 - place) + step_w * row
-        parts.append(jnp.where(place < 3, east, jnp.where(place >= 5, west, -1)))
-    return jnp.concatenate(parts, 0)
+        value = jnp.where(place < 3, east, jnp.where(place >= 5, west, -1))
+        index = jnp.where((local >= 0) & (local < 8 * side), value, index)
+    return index
+
+
+def host_of(block, size):
+    last = lax.rem(block, ROW) == ROW - 1
+    return jnp.where(last, lax.rem(block + ROW, size), block)
+
+
+def block_of(device, size):
+    last = lax.rem(device, ROW) == ROW - 1
+    return jnp.where(last, lax.rem(device + size - ROW, size), device)
 
 
 def spread_taps(weight):
@@ -135,7 +147,8 @@
         df_shrink, head_w,
     ) = vmem_weights = refs[2 : 2 + WEIGHTS]
     (
-        states_in, gru_in,
+        states_in, gru_in, states_moved, gru_moved, info_moved,
+        result_out, result_in, gru_out, gru_back,
         weather, carried, embed, gru_a, gru_b, lift_w, comb_b,
         taps_ef, taps_df, taps_ec, taps_dc,
         near0, near1, own_far, far1, far0, grow, gather, far_grow,
@@ -143,11 +156,16 @@
         part, far_part, held_gates,
         info_out, info_in, w_out, w_in, f_out, f_in, c_out, c_in,
         load,
-        info_send, info_recv, w_send, w_recv, f_send, f_recv, c_send, c_recv,
+        m_send, m_recv, r_send, r_recv, info_send, info_recv, w_send, w_recv, f_send, f_recv, c_send, c_recv,
     ) = refs[2 + WEIGHTS :]
     size = lax.axis_size("face")
     me = lax.axis_index("face")
-    after, before = lax.rem(me + 1, size), lax.rem(me + size - 1, size)
+    mine, away = block_of(me, size), host_of(me, size)
+    moved = away != me
+    own_after, own_before = (lax.rem(me + k, size) for k in (1, size - 1))
+    home_after, home_before = (lax.rem(mine + k, size) for k in (1, size - 1))
+    after, before = host_of(home_after, size), host_of(home_before, size)
+    first_targets = host_of(own_after, size), host_of(own_before, size)
 
     def remote(src, dst, send, recv, target):
         return pltpu.make_async_remote_copy(
@@ -163,15 +181,32 @@
 
     def info_copies():
         return [
-            remote(info_out.at[w], info_in.at[w], info_send.at[w], info_recv.at[w], target)
-            for w, target in enumerate((after, before))
+            remote(info_out, info_in.at[w], info_send.at[w], info_recv.at[w], target)
+            for w, target in enumerate(first_targets)
         ]
 
-    def weather_copies(step):
+    def weather_copies(step, targets):
         return [
             remote(w_out.at[step], w_in.at[step, w], w_send.at[step, w], w_recv.at[step, w], target)
-            for w, target in enumerate((after, before))
+            for w, target in enumerate(targets)
         ]
+
+    def state_copy():
+        return remote(states_in, states_moved, m_send.at[0], m_recv.at[0], away)
+
+    def own_info_copy():
+        return remote(info_out, info_moved, m_send.at[1], m_recv.at[1], away)
+
+    def gru_copy():
+        return remote(gru_in, gru_moved, m_send.at[2], m_recv.at[2], away)
+
+    def result_copy(step):
+        return remote(
+            result_out.at[step], result_in.at[step], r_send.at[step], r_recv.at[step], mine
+        )
+
+    def gru_result_copy():
+        return remote(gru_out, gru_back, m_send.at[3], m_recv.at[3], mine)
 
     def start(copies):
         for copy in copies:
@@ -182,10 +217,17 @@
             copy.wait()
 
     barrier = pltpu.get_barrier_semaphore()
-    for target in (after, before):
+    for target in (home_after, home_before, after, before):
         pl.semaphore_signal(
             barrier, inc=1, device_id={"face": target}, device_id_type=pl.DeviceIdType.MESH
         )
+
+    @pl.when(moved)
+    def _():
+        for target in (mine, away):
+            pl.semaphore_signal(
+                barrier, inc=1, device_id={"face": target}, device_id_type=pl.DeviceIdType.MESH
+            )
     loads = [pltpu.make_async_copy(states, states_in, load.at[0])]
     loads += [
         pltpu.make_async_copy(src, dst, load.at[2 + n])
@@ -194,23 +236,27 @@
     loads.append(pltpu.make_async_copy(gru_state, gru_in, load.at[1]))
     start(loads)
 
-    lane = lax.broadcasted_iota(jnp.int32, (1, 128), 1)
-    for way, p in ((0, SOUTH), (1, NORTH)):
-        info_out[way, 0:1] = far_index(lane, nbr, orient, SIDE0, p)
-        info_out[way, 1:2] = far_index(lane, nbr, orient, SIDE1, p)
-        info_out[way, 2:8] = jnp.zeros((6, 128), jnp.int32)
+    lane = lax.broadcasted_iota(jnp.int32, (1, 256), 1)
+    for row, p in ((0, NORTH), (2, SOUTH)):
+        info_out[row : row + 1] = far_index(lane, nbr, orient, SIDE0, p)
+        info_out[row + 1 : row + 2] = far_index(lane, nbr, orient, SIDE1, p)
+    info_out[4:5] = near_index(lane, nbr, orient, SIDE0)
+    info_out[5:6] = near_index(lane, nbr, orient, SIDE1)
+    info_out[6:8] = jnp.zeros((2, 256), jnp.int32)
     weather[...] = jnp.zeros_like(weather)
     loads[0].wait()
     weather[:FIELDS] = states_in[:, 0, :]
     w_out[0] = weather[...].astype(BF16)
-    pl.semaphore_wait(barrier, 2)
-    start(weather_copies(0))
+    pl.semaphore_wait(barrier, jnp.where(moved, 6, 4))
+
+    @pl.when(moved)
+    def _():
+        state_copy().start()
+        own_info_copy().start()
+
+    start(weather_copies(0, first_targets))
     start(info_copies())
 
-    near0[...] = one_hot(near_index(nbr, orient, SIDE0), CELLS0, 1).astype(BF16)
-    for way, p in ((0, NORTH), (1, SOUTH)):
-        m = lax.broadcasted_iota(jnp.int32, (RIM0, 1), 0)
-        own_far[way] = one_hot(far_index(m, nbr, orient, SIDE0, p), CELLS0, 1).astype(BF16)
     pad0[...] = jnp.zeros_like(pad0)
     halo0[...] = jnp.zeros_like(halo0)
     for copy in loads[1:]:
@@ -219,10 +265,26 @@
     embed[:FIELDS] = embed_w[...].astype(F32)
     taps_ef[...] = spread_taps(ef_depth[...])
 
+    @pl.when(moved)
+    def _():
+        gru_copy().start()
+        state_copy().wait()
+        own_info_copy().wait()
+        weather[:FIELDS] = states_moved[:, 0, :]
+
+    @pl.when(jnp.logical_not(moved))
+    def _():
+        info_moved[...] = info_out[...]
+
+    near0[...] = one_hot(info_moved[4:5], CELLS0, 0).T.astype(BF16)
+    for way in range(2):
+        wanted = info_moved[2 * way : 2 * way + 1, :128]
+        own_far[way] = one_hot(wanted, CELLS0, 0).T[:RIM0].astype(BF16)
+
     def prepare_rest():
         pad1[...] = jnp.zeros_like(pad1)
         halo1[...] = jnp.zeros_like(halo1)
-        near1[...] = one_hot(near_index(nbr, orient, SIDE1), CELLS1, 1).astype(BF16)
+        near1[...] = one_hot(info_moved[5:6, :128], CELLS1, 0).T.astype(BF16)
         taps_df[...] = spread_taps(df_depth[...])
         taps_ec[...] = spread_taps(ec_depth[...])
         taps_dc[...] = spread_taps(dc_depth[...])
@@ -245,6 +307,12 @@
         grow[:, CELLS1:] = one
         cell = lax.broadcasted_iota(jnp.int32, (1, CELLS0), 1)
         gather[:CELLS1] = (0.25 * one_hot(coarse_of(cell), CELLS1, 0)).astype(BF16)
+
+        @pl.when(moved)
+        def _():
+            gru_copy().wait()
+            gru_in[...] = gru_moved[...]
+
         state = jnp.concatenate(
             [gru_in[...].reshape(C1, CELLS1), jnp.zeros((256 - C1, CELLS1), F32)], 0
         )
@@ -252,7 +320,7 @@
 
     def prepare_sends():
         for way in range(2):
-            wanted = info_in[1 - way]
+            wanted = info_in[1 - way, 2 * way : 2 * way + 2, :128]
             rows = slice(way * RIM0, (way + 1) * RIM0)
             far0[rows] = one_hot(wanted[0:1], CELLS0, 0).T[:RIM0].astype(BF16)
             rows = slice(way * RIM1, (way + 1) * RIM1)
@@ -348,7 +416,7 @@
             wait(info_copies())
             prepare_sends()
 
-        wait(weather_copies(step))
+        wait(weather_copies(step, (after, before)))
         for way in range(2):
             rim = dot_nt(own_far[way], w_in[step, way]).astype(BF16)
             rim = dot_nn(rim, lift).astype(BF16).astype(F32)
@@ -390,7 +458,16 @@
             @pl.when(step == STEPS - 1)
             def _():
                 last = jnp.concatenate([carried[...], jnp.zeros((CELLS1, 256 - C1), F32)], 1)
-                gru_final[0] = last.T[:C1]
+                last = last.T[:C1]
+
+                @pl.when(moved)
+                def _():
+                    gru_out[...] = last
+                    gru_result_copy().start()
+
+                @pl.when(jnp.logical_not(moved))
+                def _():
+                    gru_final[0] = last
 
         decoded = coarse_block(
             new, 2 * step + 1, taps_dc, dc_expand, dc_shrink, after_update
@@ -417,12 +494,28 @@
         @pl.when(step < STEPS - 1)
         def _():
             w_out[step + 1] = weather[...].astype(BF16)
-            start(weather_copies(step + 1))
-
-        forecast[step, 0] = now
+            start(weather_copies(step + 1, (after, before)))
+
+        @pl.when(moved)
+        def _():
+            result_out[step] = weather[...]
+            result_copy(step).start()
+
+        @pl.when(jnp.logical_not(moved))
+        def _():
+            forecast[step, 0] = now
+
         return 0
 
     lax.fori_loop(0, STEPS, step_body, 0)
+
+    @pl.when(moved)
+    def _():
+        gru_result_copy().wait()
+        gru_final[0] = gru_back[...]
+        for step in range(STEPS):
+            result_copy(step).wait()
+            forecast[step, 0] = result_in[step, :FIELDS]
 
 
 def local(states, gru_state, neighbours, orient, *weights):
@@ -442,6 +535,13 @@
     scratch += [
         pltpu.VMEM((FIELDS, 1, CELLS0), F32),
         pltpu.VMEM((C1, 1, CELLS1), F32),
+        pltpu.VMEM((FIELDS, 1, CELLS0), F32),
+        pltpu.VMEM((C1, 1, CELLS1), F32),
+        pltpu.VMEM((8, 256), jnp.int32),
+        pltpu.VMEM((STEPS, ROWS, CELLS0), F32),
+        pltpu.VMEM((STEPS, ROWS, CELLS0), F32),
+        pltpu.VMEM((C1, CELLS1), F32),
+        pltpu.VMEM((C1, CELLS1), F32),
         pltpu.VMEM((ROWS, CELLS0), F32),
         pltpu.VMEM((CELLS1, C1), F32),
         pltpu.VMEM((ROWS, C0), F32),
@@ -474,8 +574,8 @@
         pltpu.VMEM((CELLS0, C0), F32),
         pltpu.VMEM((2 * RIM0, C0), F32),
         pltpu.VMEM((2, CELLS1, C1), F32),
-        pltpu.VMEM((2, 8, 128), jnp.int32),
-        pltpu.VMEM((2, 8, 128), jnp.int32),
+        pltpu.VMEM((8, 256), jnp.int32),
+        pltpu.VMEM((2, 8, 256), jnp.int32),
         pltpu.VMEM((STEPS, ROWS, CELLS0), BF16),
         pltpu.VMEM((STEPS, 2, ROWS, CELLS0), BF16),
         pltpu.VMEM((STEPS, 2, RIM0, C0), BF16),
@@ -483,6 +583,10 @@
         pltpu.VMEM((2 * STEPS, 2, RIM1, C1), BF16),
         pltpu.VMEM((2 * STEPS, 2, RIM1, C1), BF16),
         pltpu.SemaphoreType.DMA((2 + WEIGHTS,)),
+        pltpu.SemaphoreType.DMA((4,)),
+        pltpu.SemaphoreType.DMA((4,)),
+        pltpu.SemaphoreType.DMA((STEPS,)),
+        pltpu.SemaphoreType.DMA((STEPS,)),
         pltpu.SemaphoreType.DMA((2,)),
         pltpu.SemaphoreType.DMA((2,)),
         pltpu.SemaphoreType.DMA((STEPS, 2)),

time: 62.6 us -> 56.3 us (0.90)
  Pallas kernels: 59.6 us -> 53.2 us
    pallas_call x1, Pallas kernels: 59.6 us -> 53.2 us  [local(): pl.pallas_call(kernel, out_shape=(jax.ShapeDtypeStruct((STEPS, 1, FIELDS,...]
where the time goes in v2:
time: 56.3 us; the launch traced here: 56.1 us
  Pallas kernels  53.2 us (94%)
  local copies, waits for them, and re-layouts  2.26 us (4%)
  between operations  0.66 us (1%)
    pallas_call x1, Pallas kernels, local(): pl.pallas_call(kernel, out_shape=(jax.ShapeDtypeStruct((STEPS, 1, FIELDS,...  53.2 us
    pallas_call x2, local copies, waits for them, and re-layouts, local(): pl.pallas_call(kernel, out_shape=(jax.ShapeDtypeStruct((STEPS, 1, FIELDS,...  2.26 us

profile of v2, /device:TPU:16, one launch (start us, length us, event | category | flops | bytes accessed | tf_op | source)
XLA Modules:
  0.0 56.1 jit_solution(18177670381118446394)
XLA Ops:
  0.6 53.2 %shard_map.221 = (f32[2,1,9,512]{3,2,1,0:T(8,128)}, f32[1,180,128]{2,1,0:T(8,128)}) custom-call(f32[9,1,512]{2,1,0:T(1,128)} %bitcast.22, f32[180,1,128]{2,1,0:T(1,128)} %bitcast.15, s32[2,4]{1,0:T(2,128)} %nbr.1, s32[2,4]{1,0:T(2,128)} %orient.1, bf16[9,90]{1,0:T(8,128)(2,1)} %bitcast.25, bf16[49,90]{1,0:T(8,128)(2,1)} %bitcast.23, ...), custom_call_target="tpu_custom_call" | custom-call | tf_op jit(solution)/shard_map/pallas_call | solution.py:599
  53.9 0.0 copy-start
  53.9 1.5 %copy.24 = f32[2,1,9,512]{3,1,2,0:T(1,128)} copy(f32[2,1,9,512]{3,2,1,0:T(8,128)} %get-tuple-element.2) | data formatting | bytes 73728 | tf_op jit(solution)/shard_map/pallas_call | solution.py:599
  55.4 0.0 copy-done
  55.4 0.7 %copy.25 = f32[1,180,128]{2,0,1:T(1,128)} copy(f32[1,180,128]{2,1,0:T(8,128)S(1)} %copy-done) | data formatting | bytes 184320 | tf_op jit(solution)/shard_map/pallas_call | solution.py:599
Async XLA Ops:
  53.9 1.5 %copy-start = (f32[1,180,128]{2,1,0:T(8,128)S(1)}, f32[1,180,128]{2,1,0:T(8,128)}, u32[]{:S(2)}) copy-start(f32[1,180,128]{2,1,0:T(8,128)} %get-tuple-element.3) | copy-start | bytes 276484

commit v3 on v2

--- a/solution.py
+++ b/solution.py
@@ -76,14 +76,18 @@
     return index
 
 
-def host_of(block, size):
+def host_of(segment, block, size):
+    core, odd = segment & 1, block & 1
+    face = block - odd + core
     last = lax.rem(block, ROW) == ROW - 1
-    return jnp.where(last, lax.rem(block + ROW, size), block)
-
-
-def block_of(device, size):
-    last = lax.rem(device, ROW) == ROW - 1
-    return jnp.where(last, lax.rem(device + size - ROW, size), device)
+    return segment - core + odd, jnp.where(last, lax.rem(face + ROW, size), face)
+
+
+def block_of(segment, face, size):
+    core, odd = segment & 1, face & 1
+    block = face - odd + core
+    last = lax.rem(block, ROW) == ROW - 1
+    return segment - core + odd, jnp.where(last, lax.rem(block + size - ROW, size), block)
 
 
 def spread_taps(weight):
@@ -159,18 +163,29 @@
         m_send, m_recv, r_send, r_recv, info_send, info_recv, w_send, w_recv, f_send, f_recv, c_send, c_recv,
     ) = refs[2 + WEIGHTS :]
     size = lax.axis_size("face")
-    me = lax.axis_index("face")
-    mine, away = block_of(me, size), host_of(me, size)
-    moved = away != me
-    own_after, own_before = (lax.rem(me + k, size) for k in (1, size - 1))
-    home_after, home_before = (lax.rem(mine + k, size) for k in (1, size - 1))
-    after, before = host_of(home_after, size), host_of(home_before, size)
-    first_targets = host_of(own_after, size), host_of(own_before, size)
+    here = lax.axis_index("segment"), lax.axis_index("face")
+    mine = block_of(*here, size)
+    away = host_of(*here, size)
+    moved = (away[0] != here[0]) | (away[1] != here[1])
+
+    def beside(place, step):
+        return place[0], lax.rem(place[1] + step + size, size)
+
+    home_after, home_before = beside(mine, 1), beside(mine, -1)
+    after, before = host_of(*home_after, size), host_of(*home_before, size)
+    first_targets = host_of(*beside(here, 1), size), host_of(*beside(here, -1), size)
+
+    def greet(target):
+        pl.semaphore_signal(
+            barrier, inc=1, device_id={"segment": target[0], "face": target[1]},
+            device_id_type=pl.DeviceIdType.MESH,
+        )
 
     def remote(src, dst, send, recv, target):
         return pltpu.make_async_remote_copy(
             src_ref=src, dst_ref=dst, send_sem=send, recv_sem=recv,
-            device_id={"face": target}, device_id_type=pl.DeviceIdType.MESH,
+            device_id={"segment": target[0], "face": target[1]},
+            device_id_type=pl.DeviceIdType.MESH,
         )
 
     def pair(out, into, send, recv, slot):
@@ -218,16 +233,13 @@
 
     barrier = pltpu.get_barrier_semaphore()
     for target in (home_after, home_before, after, before):
-        pl.semaphore_signal(
-            barrier, inc=1, device_id={"face": target}, device_id_type=pl.DeviceIdType.MESH
-        )
+        greet(target)
 
     @pl.when(moved)
     def _():
-        for target in (mine, away):
-            pl.semaphore_signal(
-                barrier, inc=1, device_id={"face": target}, device_id_type=pl.DeviceIdType.MESH
-            )
+        greet(mine)
+        greet(away)
+
     loads = [pltpu.make_async_copy(states, states_in, load.at[0])]
     loads += [
         pltpu.make_async_copy(src, dst, load.at[2 + n])

time: 56.3 us -> 52.4 us (0.931)
  the two profiles are of different devices: /device:TPU:16 before, /device:TPU:1 now
where the time goes in v3:
time: 52.4 us; the launch traced here: 52.2 us
  Pallas kernels  49.3 us (94%)
  local copies, waits for them, and re-layouts  2.26 us (4%)
  between operations  0.66 us (1%)
    pallas_call x1, Pallas kernels, local(): pl.pallas_call(kernel, out_shape=(jax.ShapeDtypeStruct((STEPS, 1, FIELDS,...  49.3 us
    pallas_call x2, local copies, waits for them, and re-layouts, local(): pl.pallas_call(kernel, out_shape=(jax.ShapeDtypeStruct((STEPS, 1, FIELDS,...  2.26 us

profile of v3, /device:TPU:1, one launch (start us, length us, event | category | flops | bytes accessed | tf_op | source)
XLA Modules:
  0.0 52.2 jit_solution(10729710404125482924)
XLA Ops:
  0.6 49.3 %shard_map.221 = (f32[2,1,9,512]{3,2,1,0:T(8,128)}, f32[1,180,128]{2,1,0:T(8,128)}) custom-call(f32[9,1,512]{2,1,0:T(1,128)} %bitcast.22, f32[180,1,128]{2,1,0:T(1,128)} %bitcast.15, s32[2,4]{1,0:T(2,128)} %nbr.1, s32[2,4]{1,0:T(2,128)} %orient.1, bf16[9,90]{1,0:T(8,128)(2,1)} %bitcast.25, bf16[49,90]{1,0:T(8,128)(2,1)} %bitcast.23, ...), custom_call_target="tpu_custom_call" | custom-call | tf_op jit(solution)/shard_map/pallas_call | solution.py:611
  50.0 0.0 copy-start
  50.0 1.5 %copy.24 = f32[2,1,9,512]{3,1,2,0:T(1,128)} copy(f32[2,1,9,512]{3,2,1,0:T(8,128)} %get-tuple-element.2) | data formatting | bytes 73728 | tf_op jit(solution)/shard_map/pallas_call | solution.py:611
  51.5 0.0 copy-done
  51.5 0.7 %copy.25 = f32[1,180,128]{2,0,1:T(1,128)} copy(f32[1,180,128]{2,1,0:T(8,128)S(1)} %copy-done) | data formatting | bytes 184320 | tf_op jit(solution)/shard_map/pallas_call | solution.py:611
Async XLA Ops:
  50.0 1.5 %copy-start = (f32[1,180,128]{2,1,0:T(8,128)S(1)}, f32[1,180,128]{2,1,0:T(8,128)}, u32[]{:S(2)}) copy-start(f32[1,180,128]{2,1,0:T(8,128)} %get-tuple-element.3) | copy-start | bytes 276484

commit v4 on v3

--- a/solution.py
+++ b/solution.py
@@ -78,16 +78,16 @@
 
 def host_of(segment, block, size):
     core, odd = segment & 1, block & 1
-    face = block - odd + core
+    face = block - odd + (1 - core)
     last = lax.rem(block, ROW) == ROW - 1
-    return segment - core + odd, jnp.where(last, lax.rem(face + ROW, size), face)
+    return segment - core + (1 - odd), jnp.where(last, lax.rem(face + ROW, size), face)
 
 
 def block_of(segment, face, size):
     core, odd = segment & 1, face & 1
-    block = face - odd + core
+    block = face - odd + (1 - core)
     last = lax.rem(block, ROW) == ROW - 1
-    return segment - core + odd, jnp.where(last, lax.rem(block + size - ROW, size), block)
+    return segment - core + (1 - odd), jnp.where(last, lax.rem(block + size - ROW, size), block)
 
 
 def spread_taps(weight):
@@ -263,26 +263,51 @@
 
     @pl.when(moved)
     def _():
+        own_info_copy().start()
         state_copy().start()
-        own_info_copy().start()
 
     start(weather_copies(0, first_targets))
     start(info_copies())
 
+    def coarse_of(cell):
+        tile = lax.shift_right_logical(cell, 8)
+        row = lax.shift_right_logical(cell, 5) & 7
+        return tile * 64 + row * 8 + (lax.shift_right_logical(cell, 1) & 7)
+
     pad0[...] = jnp.zeros_like(pad0)
     halo0[...] = jnp.zeros_like(halo0)
+    pad1[...] = jnp.zeros_like(pad1)
+    halo1[...] = jnp.zeros_like(halo1)
+    cell = lax.broadcasted_iota(jnp.int32, (CELLS0, 1), 0)
+    one = one_hot(coarse_of(cell), CELLS1, 1).astype(BF16)
+    grow[:, :CELLS1] = one
+    grow[:, CELLS1:] = one
+    cell = lax.broadcasted_iota(jnp.int32, (1, CELLS0), 1)
+    gather[:CELLS1] = (0.25 * one_hot(coarse_of(cell), CELLS1, 0)).astype(BF16)
     for copy in loads[1:]:
         copy.wait()
+
+    @pl.when(moved)
+    def _():
+        gru_copy().start()
+
     embed[...] = jnp.zeros_like(embed)
     embed[:FIELDS] = embed_w[...].astype(F32)
     taps_ef[...] = spread_taps(ef_depth[...])
+    taps_df[...] = spread_taps(df_depth[...])
+    taps_ec[...] = spread_taps(ec_depth[...])
+    taps_dc[...] = spread_taps(dc_depth[...])
+    for g in range(3):
+        wide = gru_w[g].astype(F32)
+        gru_a[g] = wide[:, :C1].astype(BF16)
+        gru_b[g] = wide[:, C1:].astype(BF16)
+    wide = combine_w[...].astype(F32)
+    comb_b[...] = wide[C0:].astype(BF16)
+    lift_w[...] = dot_nn(up_w[...], wide[:C0].astype(BF16)).astype(BF16)
 
     @pl.when(moved)
     def _():
-        gru_copy().start()
-        state_copy().wait()
         own_info_copy().wait()
-        weather[:FIELDS] = states_moved[:, 0, :]
 
     @pl.when(jnp.logical_not(moved))
     def _():
@@ -293,32 +318,26 @@
         wanted = info_moved[2 * way : 2 * way + 1, :128]
         own_far[way] = one_hot(wanted, CELLS0, 0).T[:RIM0].astype(BF16)
 
+    @pl.when(moved)
+    def _():
+        state_copy().wait()
+        weather[:FIELDS] = states_moved[:, 0, :]
+
+    def prepare_gather():
+        for way in range(2):
+            wanted = info_in[1 - way, 2 * way + 1 : 2 * way + 2, :128]
+            rows = slice(way * RIM1, (way + 1) * RIM1)
+            far1[rows] = one_hot(wanted, CELLS1, 0).T[:RIM1].astype(BF16)
+        gather[CELLS1:] = dot_nn(far1[...], gather[:CELLS1]).astype(BF16)
+
     def prepare_rest():
-        pad1[...] = jnp.zeros_like(pad1)
-        halo1[...] = jnp.zeros_like(halo1)
-        near1[...] = one_hot(info_moved[5:6, :128], CELLS1, 0).T.astype(BF16)
-        taps_df[...] = spread_taps(df_depth[...])
-        taps_ec[...] = spread_taps(ec_depth[...])
-        taps_dc[...] = spread_taps(dc_depth[...])
-        for g in range(3):
-            wide = gru_w[g].astype(F32)
-            gru_a[g] = wide[:, :C1].astype(BF16)
-            gru_b[g] = wide[:, C1:].astype(BF16)
-        wide = combine_w[...].astype(F32)
-        comb_b[...] = wide[C0:].astype(BF16)
-        lift_w[...] = dot_nn(up_w[...], wide[:C0].astype(BF16)).astype(BF16)
-
-        def coarse_of(cell):
-            tile = lax.shift_right_logical(cell, 8)
-            row = lax.shift_right_logical(cell, 5) & 7
-            return tile * 64 + row * 8 + (lax.shift_right_logical(cell, 1) & 7)
-
-        cell = lax.broadcasted_iota(jnp.int32, (CELLS0, 1), 0)
-        one = one_hot(coarse_of(cell), CELLS1, 1).astype(BF16)
-        grow[:, :CELLS1] = one
-        grow[:, CELLS1:] = one
-        cell = lax.broadcasted_iota(jnp.int32, (1, CELLS0), 1)
-        gather[:CELLS1] = (0.25 * one_hot(coarse_of(cell), CELLS1, 0)).astype(BF16)
+        for way in range(2):
+            wanted = info_in[1 - way, 2 * way : 2 * way + 1, :128]
+            rows = slice(way * RIM0, (way + 1) * RIM0)
+            far0[rows] = one_hot(wanted, CELLS0, 0).T[:RIM0].astype(BF16)
+        one = dot_nn(far0[...], grow[:, :CELLS1]).astype(BF16)
+        far_grow[:, :CELLS1] = one
+        far_grow[:, CELLS1:] = one
 
         @pl.when(moved)
         def _():
@@ -329,18 +348,6 @@
             [gru_in[...].reshape(C1, CELLS1), jnp.zeros((256 - C1, CELLS1), F32)], 0
         )
         carried[...] = state.T[:, :C1]
-
-    def prepare_sends():
-        for way in range(2):
-            wanted = info_in[1 - way, 2 * way : 2 * way + 2, :128]
-            rows = slice(way * RIM0, (way + 1) * RIM0)
-            far0[rows] = one_hot(wanted[0:1], CELLS0, 0).T[:RIM0].astype(BF16)
-            rows = slice(way * RIM1, (way + 1) * RIM1)
-            far1[rows] = one_hot(wanted[1:2], CELLS1, 0).T[:RIM1].astype(BF16)
-        gather[CELLS1:] = dot_nn(far1[...], gather[:CELLS1]).astype(BF16)
-        one = dot_nn(far0[...], grow[:, :CELLS1]).astype(BF16)
-        far_grow[:, :CELLS1] = one
-        far_grow[:, CELLS1:] = one
 
     def fill0(r):
         pad0[:, 3 : 3 + SIDE0, 8:24, :] = r.astype(F32).reshape(TILES, SIDE0, SIDE0, C0)
@@ -424,9 +431,9 @@
 
         @pl.when(step == 0)
         def _():
-            prepare_rest()
+            near1[...] = one_hot(info_moved[5:6, :128], CELLS1, 0).T.astype(BF16)
             wait(info_copies())
-            prepare_sends()
+            prepare_gather()
 
         wait(weather_copies(step, (after, before)))
         for way in range(2):
@@ -442,6 +449,10 @@
             c_out[2 * step, way] = coarse[top : top + RIM1]
 
         def after_skip():
+            @pl.when(step == 0)
+            def _():
+                prepare_rest()
+
             kept = skip[...].reshape(CELLS0, C0)
             part[...] = dot_nn(kept, comb_b[...])
             far_part[...] = dot_nn(dot_nn(far0[...], kept).astype(BF16), comb_b[...])

time: 52.4 us -> 50.6 us (0.966)
  the two profiles are of different devices: /device:TPU:1 before, /device:TPU:16 now
where the time goes in v4:
time: 50.6 us; the launch traced here: 50.5 us
  Pallas kernels  47.6 us (94%)
  local copies, waits for them, and re-layouts  2.26 us (4%)
  between operations  0.66 us (1%)
    pallas_call x1, Pallas kernels, local(): pl.pallas_call(kernel, out_shape=(jax.ShapeDtypeStruct((STEPS, 1, FIELDS,...  47.6 us
    pallas_call x2, local copies, waits for them, and re-layouts, local(): pl.pallas_call(kernel, out_shape=(jax.ShapeDtypeStruct((STEPS, 1, FIELDS,...  2.26 us

profile of v4, /device:TPU:16, one launch (start us, length us, event | category | flops | bytes accessed | tf_op | source)
XLA Modules:
  0.0 50.5 jit_solution(17112709478608915120)
XLA Ops:
  0.6 47.6 %shard_map.221 = (f32[2,1,9,512]{3,2,1,0:T(8,128)}, f32[1,180,128]{2,1,0:T(8,128)}) custom-call(f32[9,1,512]{2,1,0:T(1,128)} %bitcast.22, f32[180,1,128]{2,1,0:T(1,128)} %bitcast.15, s32[2,4]{1,0:T(2,128)} %nbr.1, s32[2,4]{1,0:T(2,128)} %orient.1, bf16[9,90]{1,0:T(8,128)(2,1)} %bitcast.25, bf16[49,90]{1,0:T(8,128)(2,1)} %bitcast.23, ...), custom_call_target="tpu_custom_call" | custom-call | tf_op jit(solution)/shard_map/pallas_call | solution.py:622
  48.2 0.0 copy-start
  48.2 1.5 %copy.24 = f32[2,1,9,512]{3,1,2,0:T(1,128)} copy(f32[2,1,9,512]{3,2,1,0:T(8,128)} %get-tuple-element.2) | data formatting | bytes 73728 | tf_op jit(solution)/shard_map/pallas_call | solution.py:622
  49.7 0.0 copy-done
  49.7 0.7 %copy.25 = f32[1,180,128]{2,0,1:T(1,128)} copy(f32[1,180,128]{2,1,0:T(8,128)S(1)} %copy-done) | data formatting | bytes 184320 | tf_op jit(solution)/shard_map/pallas_call | solution.py:622
Async XLA Ops:
  48.2 1.5 %copy-start = (f32[1,180,128]{2,1,0:T(8,128)S(1)}, f32[1,180,128]{2,1,0:T(8,128)}, u32[]{:S(2)}) copy-start(f32[1,180,128]{2,1,0:T(8,128)} %get-tuple-element.3) | copy-start | bytes 276484

commit v5 on v4

--- a/solution.py
+++ b/solution.py
@@ -371,7 +371,7 @@
             out[tile, 3:13] = finish(y, r, expand[...], shrink[...]).reshape(10, SIDE0, C0)
             return 0
 
-        lax.fori_loop(0, TILES, body, 0)
+        lax.fori_loop(0, TILES, body, 0, unroll=True)
         for tile in range(TILES):
             for side, top in ((0, 3), (1, 16)):
                 edge_r[tile, side] = pad0[tile, top : top + 3, 8:24, :]
@@ -387,7 +387,7 @@
                         edge_y[tile, side, o, columns, :] = rows[o]
             return 0
 
-        lax.fori_loop(0, TILES, body, 0)
+        lax.fori_loop(0, TILES, body, 0, unroll=True)
         y = edge_y[...].reshape(2 * RIM0, C0)
         r = edge_r[...].reshape(2 * RIM0, C0)
         done = finish(y, r, expand[...], shrink[...]).reshape(TILES, 2, 3, SIDE0, C0)
@@ -404,7 +404,7 @@
             y1[tile] = conv_tile(pad1, tile, SIDE1, 8, taps)
             return 0
 
-        lax.fori_loop(0, TILES, body, 0)
+        lax.fori_loop(0, TILES, body, 0, unroll=True)
         meanwhile()
         wait(copies)
         for way in range(2):
@@ -419,7 +419,7 @@
                     y1[tile, top + o] = rows[o]
             return 0
 
-        lax.fori_loop(0, TILES, edge, 0)
+        lax.fori_loop(0, TILES, edge, 0, unroll=True)
         y = y1[...].reshape(CELLS1, C1)
         return finish(y, r.astype(F32), expand[...], shrink[...])
 

time: 50.6 us -> 49.4 us (0.976)
  Pallas kernels: 47.6 us -> 46.3 us
    pallas_call x1, Pallas kernels: 47.6 us -> 46.3 us  [local(): pl.pallas_call(kernel, out_shape=(jax.ShapeDtypeStruct((STEPS, 1, FIELDS,...]
where the time goes in v5:
time: 49.4 us; the launch traced here: 49.2 us
  Pallas kernels  46.3 us (94%)
  local copies, waits for them, and re-layouts  2.26 us (5%)
  between operations  0.66 us (1%)
    pallas_call x1, Pallas kernels, local(): pl.pallas_call(kernel, out_shape=(jax.ShapeDtypeStruct((STEPS, 1, FIELDS,...  46.3 us
    pallas_call x2, local copies, waits for them, and re-layouts, local(): pl.pallas_call(kernel, out_shape=(jax.ShapeDtypeStruct((STEPS, 1, FIELDS,...  2.26 us

profile of v5, /device:TPU:16, one launch (start us, length us, event | category | flops | bytes accessed | tf_op | source)
XLA Modules:
  0.0 49.2 jit_solution(7565628664297964717)
XLA Ops:
  0.6 46.3 %shard_map.221 = (f32[2,1,9,512]{3,2,1,0:T(8,128)}, f32[1,180,128]{2,1,0:T(8,128)}) custom-call(f32[9,1,512]{2,1,0:T(1,128)} %bitcast.22, f32[180,1,128]{2,1,0:T(1,128)} %bitcast.15, s32[2,4]{1,0:T(2,128)} %nbr.1, s32[2,4]{1,0:T(2,128)} %orient.1, bf16[9,90]{1,0:T(8,128)(2,1)} %bitcast.25, bf16[49,90]{1,0:T(8,128)(2,1)} %bitcast.23, ...), custom_call_target="tpu_custom_call" | custom-call | tf_op jit(solution)/shard_map/pallas_call | solution.py:622
  46.9 0.0 copy-start
  46.9 1.5 %copy.24 = f32[2,1,9,512]{3,1,2,0:T(1,128)} copy(f32[2,1,9,512]{3,2,1,0:T(8,128)} %get-tuple-element.2) | data formatting | bytes 73728 | tf_op jit(solution)/shard_map/pallas_call | solution.py:622
  48.5 0.0 copy-done
  48.5 0.7 %copy.25 = f32[1,180,128]{2,0,1:T(1,128)} copy(f32[1,180,128]{2,1,0:T(8,128)S(1)} %copy-done) | data formatting | bytes 184320 | tf_op jit(solution)/shard_map/pallas_call | solution.py:622
Async XLA Ops:
  46.9 1.5 %copy-start = (f32[1,180,128]{2,1,0:T(8,128)S(1)}, f32[1,180,128]{2,1,0:T(8,128)}, u32[]{:S(2)}) copy-start(f32[1,180,128]{2,1,0:T(8,128)} %get-tuple-element.3) | copy-start | bytes 276484

commit v6 on v5

--- a/solution.py
+++ b/solution.py
@@ -141,7 +141,7 @@
 
 
 def kernel(
-    states, gru_state, nbr, orient, *refs,
+    states, gru_state, nbr_hbm, orient_hbm, *refs,
 ):
     hbm_weights, refs = refs[:WEIGHTS], refs[WEIGHTS:]
     forecast, gru_final = refs[:2]
@@ -151,15 +151,15 @@
         df_shrink, head_w,
     ) = vmem_weights = refs[2 : 2 + WEIGHTS]
     (
-        states_in, gru_in, states_moved, gru_moved, info_moved,
-        result_out, result_in, gru_out, gru_back,
+        nbr, orient, states_in, gru_in, states_moved, gru_moved, info_moved,
+        result_out, gru_out,
         weather, carried, embed, gru_a, gru_b, lift_w, comb_b,
         taps_ef, taps_df, taps_ec, taps_dc,
-        near0, near1, own_far, far1, far0, grow, gather, far_grow,
+        near0, near1, own_far, far1, far0, grow, pool, far_pool, far_grow,
         pad0, pad1, halo0, halo1, y0, y1, edge_y, edge_r, skip, merged,
         part, far_part, held_gates,
         info_out, info_in, w_out, w_in, f_out, f_in, c_out, c_in,
-        load,
+        load, store,
         m_send, m_recv, r_send, r_recv, info_send, info_recv, w_send, w_recv, f_send, f_recv, c_send, c_recv,
     ) = refs[2 + WEIGHTS :]
     size = lax.axis_size("face")
@@ -173,6 +173,12 @@
 
     home_after, home_before = beside(mine, 1), beside(mine, -1)
     after, before = host_of(*home_after, size), host_of(*home_before, size)
+    odd = (mine[1] & 1) == 1
+    far = jnp.where(odd, 0, 1)
+    ways = (
+        (far, tuple(jnp.where(odd, a, b) for a, b in zip(after, before))),
+        (1 - far, tuple(jnp.where(odd, b, a) for a, b in zip(after, before))),
+    )
     first_targets = host_of(*beside(here, 1), size), host_of(*beside(here, -1), size)
 
     def greet(target):
@@ -191,7 +197,7 @@
     def pair(out, into, send, recv, slot):
         return [
             remote(out.at[slot, w], into.at[slot, w], send.at[slot, w], recv.at[slot, w], target)
-            for w, target in enumerate((after, before))
+            for w, target in ways
         ]
 
     def info_copies():
@@ -200,10 +206,10 @@
             for w, target in enumerate(first_targets)
         ]
 
-    def weather_copies(step, targets):
+    def weather_copies(step, ways):
         return [
             remote(w_out.at[step], w_in.at[step, w], w_send.at[step, w], w_recv.at[step, w], target)
-            for w, target in enumerate(targets)
+            for w, target in ways
         ]
 
     def state_copy():
@@ -217,11 +223,17 @@
 
     def result_copy(step):
         return remote(
-            result_out.at[step], result_in.at[step], r_send.at[step], r_recv.at[step], mine
+            result_out.at[step], forecast.at[step, 0], r_send.at[step], r_recv.at[step], mine
         )
 
     def gru_result_copy():
-        return remote(gru_out, gru_back, m_send.at[3], m_recv.at[3], mine)
+        return remote(gru_out, gru_final.at[0], m_send.at[3], m_recv.at[3], mine)
+
+    def result_store(step):
+        return pltpu.make_async_copy(result_out.at[step], forecast.at[step, 0], store.at[step])
+
+    def gru_result_store():
+        return pltpu.make_async_copy(gru_out, gru_final.at[0], store.at[STEPS])
 
     def start(copies):
         for copy in copies:
@@ -240,7 +252,11 @@
         greet(mine)
         greet(away)
 
-    loads = [pltpu.make_async_copy(states, states_in, load.at[0])]
+    loads = [
+        pltpu.make_async_copy(nbr_hbm, nbr, load.at[2 + WEIGHTS]),
+        pltpu.make_async_copy(orient_hbm, orient, load.at[3 + WEIGHTS]),
+        pltpu.make_async_copy(states, states_in, load.at[0]),
+    ]
     loads += [
         pltpu.make_async_copy(src, dst, load.at[2 + n])
         for n, (src, dst) in enumerate(zip(hbm_weights, vmem_weights))
@@ -248,6 +264,8 @@
     loads.append(pltpu.make_async_copy(gru_state, gru_in, load.at[1]))
     start(loads)
 
+    loads[0].wait()
+    loads[1].wait()
     lane = lax.broadcasted_iota(jnp.int32, (1, 256), 1)
     for row, p in ((0, NORTH), (2, SOUTH)):
         info_out[row : row + 1] = far_index(lane, nbr, orient, SIDE0, p)
@@ -256,7 +274,7 @@
     info_out[5:6] = near_index(lane, nbr, orient, SIDE1)
     info_out[6:8] = jnp.zeros((2, 256), jnp.int32)
     weather[...] = jnp.zeros_like(weather)
-    loads[0].wait()
+    loads[2].wait()
     weather[:FIELDS] = states_in[:, 0, :]
     w_out[0] = weather[...].astype(BF16)
     pl.semaphore_wait(barrier, jnp.where(moved, 6, 4))
@@ -266,7 +284,7 @@
         own_info_copy().start()
         state_copy().start()
 
-    start(weather_copies(0, first_targets))
+    start(weather_copies(0, tuple(enumerate(first_targets))))
     start(info_copies())
 
     def coarse_of(cell):
@@ -283,8 +301,8 @@
     grow[:, :CELLS1] = one
     grow[:, CELLS1:] = one
     cell = lax.broadcasted_iota(jnp.int32, (1, CELLS0), 1)
-    gather[:CELLS1] = (0.25 * one_hot(coarse_of(cell), CELLS1, 0)).astype(BF16)
-    for copy in loads[1:]:
+    pool[...] = (0.25 * one_hot(coarse_of(cell), CELLS1, 0)).astype(BF16)
+    for copy in loads[3:]:
         copy.wait()
 
     @pl.when(moved)
@@ -326,18 +344,16 @@
     def prepare_gather():
         for way in range(2):
             wanted = info_in[1 - way, 2 * way + 1 : 2 * way + 2, :128]
-            rows = slice(way * RIM1, (way + 1) * RIM1)
-            far1[rows] = one_hot(wanted, CELLS1, 0).T[:RIM1].astype(BF16)
-        gather[CELLS1:] = dot_nn(far1[...], gather[:CELLS1]).astype(BF16)
+            far1[way] = one_hot(wanted, CELLS1, 0).T[:RIM1].astype(BF16)
+            far_pool[way] = dot_nn(far1[way], pool[...]).astype(BF16)
 
     def prepare_rest():
         for way in range(2):
             wanted = info_in[1 - way, 2 * way : 2 * way + 1, :128]
-            rows = slice(way * RIM0, (way + 1) * RIM0)
-            far0[rows] = one_hot(wanted, CELLS0, 0).T[:RIM0].astype(BF16)
-        one = dot_nn(far0[...], grow[:, :CELLS1]).astype(BF16)
-        far_grow[:, :CELLS1] = one
-        far_grow[:, CELLS1:] = one
+            far0[way] = one_hot(wanted, CELLS0, 0).T[:RIM0].astype(BF16)
+            one = dot_nn(far0[way], grow[:, :CELLS1]).astype(BF16)
+            far_grow[way, :, :CELLS1] = one
+            far_grow[way, :, CELLS1:] = one
 
         @pl.when(moved)
         def _():
@@ -395,9 +411,7 @@
             out[tile, 0:3] = done[tile, 0]
             out[tile, 13:16] = done[tile, 1]
 
-    def coarse_block(r, slot, taps, expand, shrink, meanwhile):
-        copies = pair(c_out, c_in, c_send, c_recv, slot)
-        start(copies)
+    def coarse_block(r, slot, copies, taps, expand, shrink, meanwhile):
         fill1(r)
 
         def body(tile, _):
@@ -435,18 +449,21 @@
             wait(info_copies())
             prepare_gather()
 
-        wait(weather_copies(step, (after, before)))
+        wait(weather_copies(step, ways))
         for way in range(2):
             rim = dot_nt(own_far[way], w_in[step, way]).astype(BF16)
             rim = dot_nn(rim, lift).astype(BF16).astype(F32)
             halo0[way, :, :, 8:24, :] = rim.reshape(TILES, 3, SIDE0, C0)
         fine_block_outer(taps_ef, ef_expand, ef_shrink, skip)
 
-        coarse = dot_nn(gather[...], skip[...].reshape(CELLS0, C0)).astype(BF16)
+        kept = skip[...].reshape(CELLS0, C0)
+        copies = pair(c_out, c_in, c_send, c_recv, 2 * step)
+        for (way, _), copy in zip(ways, copies):
+            wanted = dot_nn(far_pool[way], kept).astype(BF16)
+            c_out[2 * step, way] = dot_nt(wanted, down_w[...]).astype(BF16)
+            copy.start()
+        coarse = dot_nn(pool[...], kept).astype(BF16)
         coarse = dot_nt(coarse, down_w[...]).astype(BF16)
-        for way in range(2):
-            top = CELLS1 + way * RIM1
-            c_out[2 * step, way] = coarse[top : top + RIM1]
 
         def after_skip():
             @pl.when(step == 0)
@@ -455,13 +472,14 @@
 
             kept = skip[...].reshape(CELLS0, C0)
             part[...] = dot_nn(kept, comb_b[...])
-            far_part[...] = dot_nn(dot_nn(far0[...], kept).astype(BF16), comb_b[...])
+            for way in range(2):
+                far_part[way] = dot_nn(dot_nn(far0[way], kept).astype(BF16), comb_b[...])
             held = carried[...].astype(BF16)
             for g in range(2):
                 held_gates[g] = dot_nt(held, gru_b[g])
 
         coarse = coarse_block(
-            coarse[:CELLS1], 2 * step, taps_ec, ec_expand, ec_shrink, after_skip
+            coarse, 2 * step, copies, taps_ec, ec_expand, ec_shrink, after_skip
         )
 
         old = carried[...]
@@ -473,35 +491,34 @@
         carried[...] = new
 
         new = new.astype(BF16)
-        wanted = dot_nn(far1[...], new).astype(BF16)
-        for way in range(2):
-            c_out[2 * step + 1, way] = wanted[way * RIM1 : (way + 1) * RIM1]
+        copies = pair(c_out, c_in, c_send, c_recv, 2 * step + 1)
+        for (way, _), copy in zip(ways, copies):
+            c_out[2 * step + 1, way] = dot_nn(far1[way], new).astype(BF16)
+            copy.start()
 
         def after_update():
             @pl.when(step == STEPS - 1)
             def _():
                 last = jnp.concatenate([carried[...], jnp.zeros((CELLS1, 256 - C1), F32)], 1)
-                last = last.T[:C1]
+                gru_out[...] = last.T[:C1]
 
                 @pl.when(moved)
                 def _():
-                    gru_out[...] = last
                     gru_result_copy().start()
 
                 @pl.when(jnp.logical_not(moved))
                 def _():
-                    gru_final[0] = last
+                    gru_result_store().start()
 
         decoded = coarse_block(
-            new, 2 * step + 1, taps_dc, dc_expand, dc_shrink, after_update
+            new, 2 * step + 1, copies, taps_dc, dc_expand, dc_shrink, after_update
         )
 
         lifted = halves(dot_nn(decoded, lift_w[...]))
-        wanted = (dot_nn(far_grow[...], lifted) + far_part[...]).astype(BF16)
-        for way in range(2):
-            f_out[step, way] = wanted[way * RIM0 : (way + 1) * RIM0]
         copies = pair(f_out, f_in, f_send, f_recv, step)
-        start(copies)
+        for (way, _), copy in zip(ways, copies):
+            f_out[step, way] = (dot_nn(far_grow[way], lifted) + far_part[way]).astype(BF16)
+            copy.start()
         fill0((dot_nn(grow[...], lifted) + part[...]).astype(BF16))
         fine_block_inner(taps_df, df_expand, df_shrink, merged)
         wait(copies)
@@ -517,16 +534,17 @@
         @pl.when(step < STEPS - 1)
         def _():
             w_out[step + 1] = weather[...].astype(BF16)
-            start(weather_copies(step + 1, (after, before)))
+            start(weather_copies(step + 1, ways))
+
+        result_out[step] = now
 
         @pl.when(moved)
         def _():
-            result_out[step] = weather[...]
             result_copy(step).start()
 
         @pl.when(jnp.logical_not(moved))
         def _():
-            forecast[step, 0] = now
+            result_store(step).start()
 
         return 0
 
@@ -535,10 +553,14 @@
     @pl.when(moved)
     def _():
         gru_result_copy().wait()
-        gru_final[0] = gru_back[...]
         for step in range(STEPS):
             result_copy(step).wait()
-            forecast[step, 0] = result_in[step, :FIELDS]
+
+    @pl.when(jnp.logical_not(moved))
+    def _():
+        gru_result_store().wait()
+        for step in range(STEPS):
+            result_store(step).wait()
 
 
 def local(states, gru_state, neighbours, orient, *weights):
@@ -553,17 +575,16 @@
         df_shrink, head_w,
     )
     hbm = pl.BlockSpec(memory_space=pltpu.HBM)
-    smem = pl.BlockSpec(memory_space=pltpu.SMEM)
     scratch = [pltpu.VMEM(w.shape, w.dtype) for w in weights]
     scratch += [
+        pltpu.SMEM((TILES, 4), jnp.int32),
+        pltpu.SMEM((TILES, 4), jnp.int32),
         pltpu.VMEM((FIELDS, 1, CELLS0), F32),
         pltpu.VMEM((C1, 1, CELLS1), F32),
         pltpu.VMEM((FIELDS, 1, CELLS0), F32),
         pltpu.VMEM((C1, 1, CELLS1), F32),
         pltpu.VMEM((8, 256), jnp.int32),
-        pltpu.VMEM((STEPS, ROWS, CELLS0), F32),
-        pltpu.VMEM((STEPS, ROWS, CELLS0), F32),
-        pltpu.VMEM((C1, CELLS1), F32),
+        pltpu.VMEM((STEPS, FIELDS, CELLS0), F32),
         pltpu.VMEM((C1, CELLS1), F32),
         pltpu.VMEM((ROWS, CELLS0), F32),
         pltpu.VMEM((CELLS1, C1), F32),
@@ -579,11 +600,12 @@
         pltpu.VMEM((TILES * SIDE0 * 8, CELLS0), BF16),
         pltpu.VMEM((TILES * SIDE1 * 8, CELLS1), BF16),
         pltpu.VMEM((2, RIM0, CELLS0), BF16),
-        pltpu.VMEM((2 * RIM1, CELLS1), BF16),
-        pltpu.VMEM((2 * RIM0, CELLS0), BF16),
+        pltpu.VMEM((2, RIM1, CELLS1), BF16),
+        pltpu.VMEM((2, RIM0, CELLS0), BF16),
         pltpu.VMEM((CELLS0, 2 * CELLS1), BF16),
-        pltpu.VMEM((CELLS1 + 2 * RIM1, CELLS0), BF16),
-        pltpu.VMEM((2 * RIM0, 2 * CELLS1), BF16),
+        pltpu.VMEM((CELLS1, CELLS0), BF16),
+        pltpu.VMEM((2, RIM1, CELLS0), BF16),
+        pltpu.VMEM((2, RIM0, 2 * CELLS1), BF16),
         pltpu.VMEM((TILES, SIDE0 + 6, 32, C0), F32),
         pltpu.VMEM((TILES, SIDE1 + 6, 24, C1), F32),
         pltpu.VMEM((2, TILES, 3, 32, C0), F32),
@@ -595,7 +617,7 @@
         pltpu.VMEM((TILES, SIDE0, SIDE0, C0), BF16),
         pltpu.VMEM((TILES, SIDE0, SIDE0, C0), BF16),
         pltpu.VMEM((CELLS0, C0), F32),
-        pltpu.VMEM((2 * RIM0, C0), F32),
+        pltpu.VMEM((2, RIM0, C0), F32),
         pltpu.VMEM((2, CELLS1, C1), F32),
         pltpu.VMEM((8, 256), jnp.int32),
         pltpu.VMEM((2, 8, 256), jnp.int32),
@@ -605,7 +627,8 @@
         pltpu.VMEM((STEPS, 2, RIM0, C0), BF16),
         pltpu.VMEM((2 * STEPS, 2, RIM1, C1), BF16),
         pltpu.VMEM((2 * STEPS, 2, RIM1, C1), BF16),
-        pltpu.SemaphoreType.DMA((2 + WEIGHTS,)),
+        pltpu.SemaphoreType.DMA((4 + WEIGHTS,)),
+        pltpu.SemaphoreType.DMA((STEPS + 1,)),
         pltpu.SemaphoreType.DMA((4,)),
         pltpu.SemaphoreType.DMA((4,)),
         pltpu.SemaphoreType.DMA((STEPS,)),
@@ -625,8 +648,8 @@
             jax.ShapeDtypeStruct((STEPS, 1, FIELDS, CELLS0), F32),
             jax.ShapeDtypeStruct((1, C1, CELLS1), F32),
         ),
-        in_specs=[hbm, hbm, smem, smem] + [hbm] * len(weights),
-        out_specs=(pl.BlockSpec(memory_space=pltpu.VMEM),) * 2,
+        in_specs=[hbm] * (4 + len(weights)),
+        out_specs=(hbm, hbm),
         scratch_shapes=scratch,
         compiler_params=pltpu.CompilerParams(
             collective_id=0, has_side_effects=True, vmem_limit_bytes=56 * 1024 * 1024

time: 49.4 us -> 48.9 us (0.990)
  no operation moved by 1% of the time
where the time goes in v6:
time: 48.9 us; the launch traced here: 48.8 us
  Pallas kernels  45.9 us (94%)
  local copies, waits for them, and re-layouts  2.26 us (5%)
  between operations  0.66 us (1%)
    pallas_call x1, Pallas kernels, local(): pl.pallas_call(kernel, out_shape=(jax.ShapeDtypeStruct((STEPS, 1, FIELDS,...  45.9 us
    pallas_call x2, local copies, waits for them, and re-layouts, local(): pl.pallas_call(kernel, out_shape=(jax.ShapeDtypeStruct((STEPS, 1, FIELDS,...  2.26 us

profile of v6, /device:TPU:16, one launch (start us, length us, event | category | flops | bytes accessed | tf_op | source)
XLA Modules:
  0.0 48.8 jit_solution(9287669607785912025)
XLA Ops:
  0.6 45.9 %shard_map.221 = (f32[2,1,9,512]{3,2,1,0:T(8,128)}, f32[1,180,128]{2,1,0:T(8,128)}) custom-call(f32[9,1,512]{2,1,0:T(1,128)} %bitcast.22, f32[180,1,128]{2,1,0:T(1,128)} %bitcast.15, s32[2,4]{1,0:T(2,128)} %nbr_hbm.1, s32[2,4]{1,0:T(2,128)} %orient_hbm.1, bf16[9,90]{1,0:T(8,128)(2,1)} %bitcast.25, bf16[49,90]{1,0:T(8,128)(2,1)} %bitcast.23, ...), custom_call_target="tpu_custom_call" | custom-call | tf_op jit(solution)/shard_map/pallas_call | solution.py:645
  46.5 0.0 copy-start
  46.5 1.5 %copy.24 = f32[2,1,9,512]{3,1,2,0:T(1,128)} copy(f32[2,1,9,512]{3,2,1,0:T(8,128)} %get-tuple-element.2) | data formatting | bytes 73728 | tf_op jit(solution)/shard_map/pallas_call | solution.py:645
  48.1 0.0 copy-done
  48.1 0.7 %copy.25 = f32[1,180,128]{2,0,1:T(1,128)} copy(f32[1,180,128]{2,1,0:T(8,128)S(1)} %copy-done) | data formatting | bytes 184320 | tf_op jit(solution)/shard_map/pallas_call | solution.py:645
Async XLA Ops:
  46.5 1.5 %copy-start = (f32[1,180,128]{2,1,0:T(8,128)S(1)}, f32[1,180,128]{2,1,0:T(8,128)}, u32[]{:S(2)}) copy-start(f32[1,180,128]{2,1,0:T(8,128)} %get-tuple-element.3) | copy-start | bytes 276484

commit v7 on v6

--- a/solution.py
+++ b/solution.py
@@ -116,13 +116,16 @@
 
 
 def conv_tile(pad, tile, rows, first, taps):
-    total = None
+    total = [None] * rows
     for q in range(7):
-        x = pad[tile, :, first + q - 3 : first + q + 5, :]
+        x = pad[tile, 3 : 3 + rows, first + q - 3 : first + q + 5, :]
         for u in range(7):
-            term = taps[7 * u + q][None] * x[u : u + rows]
-            total = term if total is None else total + term
-    return total
+            low, high = max(0, 3 - u), min(rows, rows + 3 - u)
+            term = taps[7 * u + q][None] * x[low + u - 3 : high + u - 3]
+            for o in range(low, high):
+                one = term[o - low]
+                total[o] = one if total[o] is None else total[o] + one
+    return jnp.stack(total, 0)
 
 
 def conv_halo(halo, side, tile, first, taps, rows):
@@ -262,7 +265,7 @@
         for n, (src, dst) in enumerate(zip(hbm_weights, vmem_weights))
     ]
     loads.append(pltpu.make_async_copy(gru_state, gru_in, load.at[1]))
-    start(loads)
+    start(loads[:3])
 
     loads[0].wait()
     loads[1].wait()
@@ -286,6 +289,7 @@
 
     start(weather_copies(0, tuple(enumerate(first_targets))))
     start(info_copies())
+    start(loads[3:])
 
     def coarse_of(cell):
         tile = lax.shift_right_logical(cell, 8)
@@ -378,16 +382,14 @@
         pad1[:, 3 : 3 + SIDE1, 16:24, :] = sides
 
     def fine_block_inner(taps, expand, shrink, out):
-        def body(tile, _):
+        for tile in range(TILES):
             for half in range(2):
                 total = conv_tile(pad0, tile, SIDE0, 8 + 8 * half, taps)
                 y0[tile, :, 8 * half : 8 * half + 8, :] = total
-            y = y0[tile, 3:13].reshape(10 * SIDE0, C0)
-            r = pad0[tile, 6:16, 8:24, :].reshape(10 * SIDE0, C0)
-            out[tile, 3:13] = finish(y, r, expand[...], shrink[...]).reshape(10, SIDE0, C0)
-            return 0
-
-        lax.fori_loop(0, TILES, body, 0, unroll=True)
+        y = y0[:, 3:13].reshape(TILES * 10 * SIDE0, C0)
+        r = pad0[:, 6:16, 8:24, :].reshape(TILES * 10 * SIDE0, C0)
+        done = finish(y, r, expand[...], shrink[...])
+        out[:, 3:13] = done.reshape(TILES, 10, SIDE0, C0)
         for tile in range(TILES):
             for side, top in ((0, 3), (1, 16)):
                 edge_r[tile, side] = pad0[tile, top : top + 3, 8:24, :]

time: 48.9 us -> 48.5 us (level)
  Pallas kernels: 45.9 us -> 45.4 us
    pallas_call x1, Pallas kernels: 45.9 us -> 45.4 us  [local(): pl.pallas_call(kernel, out_shape=(jax.ShapeDtypeStruct((STEPS, 1, FIELDS,...]
where the time goes in v7:
time: 48.5 us; the launch traced here: 48.3 us
  Pallas kernels  45.4 us (94%)
  local copies, waits for them, and re-layouts  2.26 us (5%)
  between operations  0.66 us (1%)
    pallas_call x1, Pallas kernels, local(): pl.pallas_call(kernel, out_shape=(jax.ShapeDtypeStruct((STEPS, 1, FIELDS,...  45.4 us
    pallas_call x2, local copies, waits for them, and re-layouts, local(): pl.pallas_call(kernel, out_shape=(jax.ShapeDtypeStruct((STEPS, 1, FIELDS,...  2.26 us

profile of v7, /device:TPU:16, one launch (start us, length us, event | category | flops | bytes accessed | tf_op | source)
XLA Modules:
  0.0 48.3 jit_solution(12762038274464453643)
XLA Ops:
  0.6 45.4 %shard_map.221 = (f32[2,1,9,512]{3,2,1,0:T(8,128)}, f32[1,180,128]{2,1,0:T(8,128)}) custom-call(f32[9,1,512]{2,1,0:T(1,128)} %bitcast.22, f32[180,1,128]{2,1,0:T(1,128)} %bitcast.15, s32[2,4]{1,0:T(2,128)} %nbr_hbm.1, s32[2,4]{1,0:T(2,128)} %orient_hbm.1, bf16[9,90]{1,0:T(8,128)(2,1)} %bitcast.25, bf16[49,90]{1,0:T(8,128)(2,1)} %bitcast.23, ...), custom_call_target="tpu_custom_call" | custom-call | tf_op jit(solution)/shard_map/pallas_call | solution.py:647
  46.0 0.0 copy-start
  46.0 1.5 %copy.24 = f32[2,1,9,512]{3,1,2,0:T(1,128)} copy(f32[2,1,9,512]{3,2,1,0:T(8,128)} %get-tuple-element.2) | data formatting | bytes 73728 | tf_op jit(solution)/shard_map/pallas_call | solution.py:647
  47.6 0.0 copy-done
  47.6 0.7 %copy.25 = f32[1,180,128]{2,0,1:T(1,128)} copy(f32[1,180,128]{2,1,0:T(8,128)S(1)} %copy-done) | data formatting | bytes 184320 | tf_op jit(solution)/shard_map/pallas_call | solution.py:647
Async XLA Ops:
  46.0 1.5 %copy-start = (f32[1,180,128]{2,1,0:T(8,128)S(1)}, f32[1,180,128]{2,1,0:T(8,128)}, u32[]{:S(2)}) copy-start(f32[1,180,128]{2,1,0:T(8,128)} %get-tuple-element.3) | copy-start | bytes 276484

commit v8 on v7

--- a/solution.py
+++ b/solution.py
@@ -146,13 +146,12 @@
 def kernel(
     states, gru_state, nbr_hbm, orient_hbm, *refs,
 ):
-    hbm_weights, refs = refs[:WEIGHTS], refs[WEIGHTS:]
-    forecast, gru_final = refs[:2]
     (
         embed_w, ef_depth, ef_expand, ef_shrink, down_w, ec_depth, ec_expand, ec_shrink,
         gru_w, dc_depth, dc_expand, dc_shrink, up_w, combine_w, df_depth, df_expand,
         df_shrink, head_w,
-    ) = vmem_weights = refs[2 : 2 + WEIGHTS]
+    ) = refs[:WEIGHTS]
+    forecast, gru_final = refs[WEIGHTS : WEIGHTS + 2]
     (
         nbr, orient, states_in, gru_in, states_moved, gru_moved, info_moved,
         result_out, gru_out,
@@ -256,13 +255,9 @@
         greet(away)
 
     loads = [
-        pltpu.make_async_copy(nbr_hbm, nbr, load.at[2 + WEIGHTS]),
-        pltpu.make_async_copy(orient_hbm, orient, load.at[3 + WEIGHTS]),
+        pltpu.make_async_copy(nbr_hbm, nbr, load.at[2]),
+        pltpu.make_async_copy(orient_hbm, orient, load.at[3]),
         pltpu.make_async_copy(states, states_in, load.at[0]),
-    ]
-    loads += [
-        pltpu.make_async_copy(src, dst, load.at[2 + n])
-        for n, (src, dst) in enumerate(zip(hbm_weights, vmem_weights))
     ]
     loads.append(pltpu.make_async_copy(gru_state, gru_in, load.at[1]))
     start(loads[:3])
@@ -577,8 +572,7 @@
         df_shrink, head_w,
     )
     hbm = pl.BlockSpec(memory_space=pltpu.HBM)
-    scratch = [pltpu.VMEM(w.shape, w.dtype) for w in weights]
-    scratch += [
+    scratch = [
         pltpu.SMEM((TILES, 4), jnp.int32),
         pltpu.SMEM((TILES, 4), jnp.int32),
         pltpu.VMEM((FIELDS, 1, CELLS0), F32),
@@ -629,7 +623,7 @@
         pltpu.VMEM((STEPS, 2, RIM0, C0), BF16),
         pltpu.VMEM((2 * STEPS, 2, RIM1, C1), BF16),
         pltpu.VMEM((2 * STEPS, 2, RIM1, C1), BF16),
-        pltpu.SemaphoreType.DMA((4 + WEIGHTS,)),
+        pltpu.SemaphoreType.DMA((4,)),
         pltpu.SemaphoreType.DMA((STEPS + 1,)),
         pltpu.SemaphoreType.DMA((4,)),
         pltpu.SemaphoreType.DMA((4,)),
@@ -650,7 +644,7 @@
             jax.ShapeDtypeStruct((STEPS, 1, FIELDS, CELLS0), F32),
             jax.ShapeDtypeStruct((1, C1, CELLS1), F32),
         ),
-        in_specs=[hbm] * (4 + len(weights)),
+        in_specs=[hbm] * 4 + [pl.BlockSpec(memory_space=pltpu.VMEM)] * len(weights),
         out_specs=(hbm, hbm),
         scratch_shapes=scratch,
         compiler_params=pltpu.CompilerParams(

time: 48.5 us -> 49.8 us (1.027)
  Pallas kernels: 45.4 us -> 46.7 us
    pallas_call x1, Pallas kernels: 45.4 us -> 46.7 us  [local(): pl.pallas_call(kernel, out_shape=(jax.ShapeDtypeStruct((STEPS, 1, FIELDS,...]
where the time goes in v8:
time: 49.8 us; the launch traced here: 49.6 us
  Pallas kernels  46.7 us (94%)
  local copies, waits for them, and re-layouts  2.26 us (5%)
  between operations  0.66 us (1%)
    pallas_call x1, Pallas kernels, local(): pl.pallas_call(kernel, out_shape=(jax.ShapeDtypeStruct((STEPS, 1, FIELDS,...  46.7 us
    pallas_call x2, local copies, waits for them, and re-layouts, local(): pl.pallas_call(kernel, out_shape=(jax.ShapeDtypeStruct((STEPS, 1, FIELDS,...  2.26 us

profile of v8, /device:TPU:16, one launch (start us, length us, event | category | flops | bytes accessed | tf_op | source)
XLA Modules:
  0.0 49.6 jit_solution(5335847756093032153)
XLA Ops:
  0.6 46.7 %shard_map.221 = (f32[2,1,9,512]{3,2,1,0:T(8,128)}, f32[1,180,128]{2,1,0:T(8,128)}) custom-call(f32[9,1,512]{2,1,0:T(1,128)} %bitcast.22, f32[180,1,128]{2,1,0:T(1,128)} %bitcast.15, s32[2,4]{1,0:T(2,128)} %nbr_hbm.1, s32[2,4]{1,0:T(2,128)} %orient_hbm.1, bf16[9,90]{1,0:T(8,128)(2,1)} %bitcast.25, bf16[49,90]{1,0:T(8,128)(2,1)} %bitcast.23, ...), custom_call_target="tpu_custom_call" | custom-call | tf_op jit(solution)/shard_map/pallas_call | solution.py:641
  47.3 0.0 copy-start
  47.3 1.5 %copy.24 = f32[2,1,9,512]{3,1,2,0:T(1,128)} copy(f32[2,1,9,512]{3,2,1,0:T(8,128)} %get-tuple-element.2) | data formatting | bytes 73728 | tf_op jit(solution)/shard_map/pallas_call | solution.py:641
  48.9 0.0 copy-done
  48.9 0.7 %copy.25 = f32[1,180,128]{2,0,1:T(1,128)} copy(f32[1,180,128]{2,1,0:T(8,128)S(1)} %copy-done) | data formatting | bytes 184320 | tf_op jit(solution)/shard_map/pallas_call | solution.py:641
Async XLA Ops:
  47.3 1.5 %copy-start = (f32[1,180,128]{2,1,0:T(8,128)S(1)}, f32[1,180,128]{2,1,0:T(8,128)}, u32[]{:S(2)}) copy-start(f32[1,180,128]{2,1,0:T(8,128)} %get-tuple-element.3) | copy-start | bytes 276484
